TPU v7x, 32 devices: a whole 2x2x4 slice. The times are simulated.
32 devices in a mesh: dp: 4 (over z), dom: 8 (over y, x, core).
Axes of the slice: x: 2, y: 2, z: 4, core: 2. Of those that a mesh axis runs over, the one named last changes fastest.
Arguments:
- grad_out: bfloat16 [4, 24, 512, 256], P('dp', 'dom'), may hold values from -6 to 6
- pre_act: bfloat16 [4, 24, 512, 256], P('dp', 'dom'), may hold values from -6 to 6
- conv_weight: bfloat16 [27, 256, 256], replicated, may hold values from -0.078125 to 0.078125
- down_weight: bfloat16 [8, 128, 256], replicated, may hold values from -0.1875 to 0.1875
- fine_act: bfloat16 [4, 192, 512, 128], P('dp', 'dom'), may hold values from -6 to 6
- neighbours: int32 [4, 24, 27], P('dp', 'dom'), may hold values from -1 to 2, as said below
- octant_routes: int32 [4, 8, 3, 8], P('dp', 'dom'), may hold values from -1 to 23, as said below
Outputs:
- fine_grad: bfloat16 [4, 192, 512, 128], P('dp', 'dom')
- conv_weight_grad: float32 [6912, 256], P('dp')
- down_weight_grad: float32 [1024, 256], P('dp')
Inputs may be any that keep to these rules, and one draw needn't show every extreme that they name: `neighbours`: each device of a scene group has between half of 3 (rounded up) and 3 live slots, always the first ones, and some device of each scene group has all 3 live. A live slot's entry 13 is itself; entry 9(a+1)+3(b+1)+(c+1) is the slot, on the device a steps along dom, of the block displaced by (a, b, c) block edges within a slab of 3 x 3 positions, or -1 where that block is empty or outside the scene group; dead slots hold -1 in all 27 entries; the relation is symmetric. `octant_routes`: row (d, k) lists what device d sends to the device d + k - 1 along dom, taken cyclically: entries 8 s + o name octant o of slot s; each live slot's 8 octants stand together, in order, in exactly one row; live entries come first, then -1. A row holds at most 8 entries, and some row of the fullest device holds exactly 8. Dead slots are never named.
All inputs are finite; a program needn't handle non-finite values.
Results may differ from a plain program's by a relative error of at most 0.0065.
Values may be sent and summed in bfloat16 or wider, within the bound.
No kernel may reach another device: no remote copies, remote signals or barrier semaphores. Data moves between devices by JAX's collectives and lax.ppermute only.
A program may use at most 128 MiB of HBM per device.

v0:
```python
import math

import jax
import jax.numpy as jnp
from jax import lax
from jax.sharding import PartitionSpec as P

BE = 8


def extended_2(block, sides, width):
    for axis, dim in sides:
        count = lax.axis_size(axis)
        forward = [(i, i + 1) for i in range(count - 1)]
        backward = [(target, source) for source, target in forward]
        low = lax.ppermute(
            lax.slice_in_dim(block, block.shape[dim] - width, None, axis=dim), axis, forward
        )
        high = lax.ppermute(lax.slice_in_dim(block, 0, width, axis=dim), axis, backward)
        block = jnp.concatenate([low, block, high], axis=dim)
    return block


def passed_along(value, axis, steps):
    count = lax.axis_size(axis)
    pairs = [(source, (source + steps) % count) for source in range(count)]
    return lax.ppermute(value, axis, pairs)


def pick_rows(source, slot_index):
    extended = jnp.concatenate([source, jnp.zeros_like(source[:1])], axis=0)
    return extended[jnp.where(slot_index < 0, source.shape[0], slot_index)]


def assemble(own_blocks, lower_faces, upper_faces, block_links):
    block_edge = own_blocks.shape[1]
    sources = (lower_faces, own_blocks, upper_faces)
    ranges = ((block_edge - 1, block_edge), (0, block_edge), (0, 1))
    parts_x = []
    for shift_x in range(3):
        parts_y = []
        for shift_y in range(3):
            parts_z = []
            for shift_z in range(3):
                links = block_links[:, 9 * shift_x + 3 * shift_y + shift_z]
                if shift_x == 1 and shift_y == 1 and (shift_z == 1):
                    portion = jnp.where(
                        (links >= 0)[:, None, None, None, None],
                        own_blocks,
                        jnp.zeros_like(own_blocks),
                    )
                else:
                    cut = sources[shift_x][
                        :,
                        :,
                        ranges[shift_y][0] : ranges[shift_y][1],
                        ranges[shift_z][0] : ranges[shift_z][1],
                    ]
                    portion = pick_rows(cut, links)
                parts_z.append(portion)
            parts_y.append(jnp.concatenate(parts_z, axis=3))
        parts_x.append(jnp.concatenate(parts_y, axis=2))
    return jnp.concatenate(parts_x, axis=1)


def correlate(grad_pad, act_pad, weight):
    block_edge = grad_pad.shape[1] - 2
    channels = grad_pad.shape[-1]
    count_blocks = grad_pad.shape[0]
    span = block_edge + 2

    def window(padded, start_x, start_y, start_z):
        return padded[
            :,
            start_x : start_x + block_edge,
            start_y : start_y + block_edge,
            start_z : start_z + block_edge,
        ].reshape(-1, channels)

    centre_grad = window(grad_pad, 1, 1, 1)
    slabs = [
        grad_pad[:, 1 - tap_x : 1 - tap_x + block_edge].reshape(-1, channels)
        for tap_x in (-1, 0, 1)
    ]
    input_grad = jnp.zeros(
        (count_blocks, block_edge, block_edge, block_edge, weight.shape[1]), jnp.float32
    )
    for tap_y in (-1, 0, 1):
        for tap_z in (-1, 0, 1):
            plane_sum = jnp.zeros((slabs[0].shape[0], weight.shape[1]), jnp.float32)
            for index_x in range(3):
                position = 9 * index_x + 3 * (tap_y + 1) + (tap_z + 1)
                plane_sum = plane_sum + lax.dot_general(
                    slabs[index_x],
                    weight[position],
                    (((1,), (1,)), ((), ())),
                    preferred_element_type=jnp.float32,
                )
            plane_sum = plane_sum.reshape(count_blocks, block_edge, span, span, weight.shape[1])
            input_grad = (
                input_grad
                + plane_sum[
                    :, :, 1 - tap_y : 1 - tap_y + block_edge, 1 - tap_z : 1 - tap_z + block_edge
                ]
            )
    weight_grads = []
    for position in range(27):
        tap_x = position // 9 - 1
        tap_y = position // 3 % 3 - 1
        tap_z = position % 3 - 1
        weight_grads.append(
            lax.dot_general(
                window(act_pad, 1 + tap_x, 1 + tap_y, 1 + tap_z),
                centre_grad,
                (((0,), (0,)), ((), ())),
                preferred_element_type=jnp.float32,
            )
        )
    return (input_grad.reshape(-1, weight.shape[1]), jnp.stack(weight_grads))


def split_octants(blocks):
    count_blocks = blocks.shape[0]
    half_edge = blocks.shape[1] // 2
    channels = blocks.shape[-1]
    parted = blocks.reshape(count_blocks, 2, half_edge, 2, half_edge, 2, half_edge, channels)
    parted = parted.transpose(0, 1, 3, 5, 2, 4, 6, 7)
    return parted.reshape(count_blocks * 8, half_edge * half_edge * half_edge, channels)


def body(grad_out, pre_act, conv_weight, down_weight, fine_act, neighbours, octant_routes):
    slot_total = grad_out.shape[1]
    voxels = grad_out.shape[2]
    channels = grad_out.shape[3]
    grad_blocks = grad_out[0].reshape(slot_total, BE, BE, BE, channels)
    act_blocks = jnp.maximum(pre_act[0], 0).reshape(slot_total, BE, BE, BE, channels)
    block_links = neighbours[0]
    faces = jnp.stack(
        [
            jnp.stack([grad_blocks[:, 0], grad_blocks[:, BE - 1]]),
            jnp.stack([act_blocks[:, 0], act_blocks[:, BE - 1]]),
        ]
    )
    widened = extended_2(faces, (("dom", 1),), 1)
    lower_faces = widened[:, 0][:, :, None]
    upper_faces = widened[:, 3][:, :, None]
    grad_pad = assemble(grad_blocks, lower_faces[0], upper_faces[0], block_links)
    act_pad = assemble(act_blocks, lower_faces[1], upper_faces[1], block_links)
    input_grad, conv_part = correlate(grad_pad, act_pad, conv_weight)
    grad_in = jnp.where(pre_act[0].reshape(-1, channels) > 0, input_grad, 0.0).astype(jnp.bfloat16)
    octants = split_octants(grad_in.reshape(slot_total, BE, BE, BE, channels))
    octant_voxels = octants.shape[1]
    peer_places = octant_routes.shape[-1]
    outgoing = pick_rows(octants, octant_routes[0, 0].reshape(-1)).reshape(
        3, peer_places, octant_voxels, channels
    )
    from_upper = passed_along(outgoing[0], "dom", -1)
    from_lower = passed_along(outgoing[2], "dom", 1)
    arrived = jnp.stack([from_upper, outgoing[1], from_lower])
    octant_grad = arrived.reshape(-1, octant_voxels, channels)
    fine_split = fine_act[0].reshape(fine_act.shape[1], 8, octant_voxels, fine_act.shape[3])
    fine_grad = jnp.einsum(
        "fcj,qij->fqci", octant_grad, down_weight, preferred_element_type=jnp.float32
    )
    fine_grad = fine_grad.astype(jnp.bfloat16).reshape(fine_act.shape)
    down_part = jnp.einsum(
        "fqci,fcj->qij", fine_split, octant_grad, preferred_element_type=jnp.float32
    )
    conv_part = conv_part.reshape(-1, channels)
    down_part = down_part.reshape(-1, channels)
    factor = 1.0 / math.sqrt(lax.axis_size("dp") * lax.axis_size("dom") * slot_total * voxels)
    conv_sum, down_sum = lax.psum((conv_part, down_part), ("dp", "dom"))
    data_index = lax.axis_index("dp")
    data_length = lax.axis_size("dp")
    conv_rows = conv_sum.shape[0] // data_length
    down_rows = down_sum.shape[0] // data_length
    conv_sum = lax.dynamic_slice_in_dim(conv_sum, data_index * conv_rows, conv_rows, 0)
    down_sum = lax.dynamic_slice_in_dim(down_sum, data_index * down_rows, down_rows, 0)
    return (fine_grad, conv_sum * factor, down_sum * factor)


def solution(mesh):
    return jax.shard_map(
        body,
        mesh=mesh,
        in_specs=(
            P("dp", "dom", None, None),
            P("dp", "dom", None, None),
            P(),
            P(),
            P("dp", "dom", None, None),
            P("dp", "dom", None),
            P("dp", "dom", None, None),
        ),
        out_specs=(P("dp", "dom", None, None), P("dp", None), P("dp", None)),
        check_vma=False,
    )
```

profile of v0, /device:TPU:0, one launch (start us, length us, event | category | flops | bytes accessed | tf_op | source)
XLA Modules:
  0.0 591.6 jit_solution(13164447402416298960)
XLA Ops:
  11.9 3.7 collective-permute-start.1
  43.2 2.7 broadcast_select_fusion
  56.8 2.2 gather_fusion.1
  59.0 3.7 maximum_maximum_fusion.2
  62.7 3.6 reshape.154
  66.3 2.2 gt.12
  83.2 2.2 gather_fusion.37
  97.0 4.9 maximum_maximum_fusion.4
  129.1 2.2 gather_fusion.12
  133.3 6.3 %fusion.6 = bf16[3,8,10,10,256]{4,3,2,1,0:T(8,128)(2,1)} fusion(bf16[3,1,1,1,256]{4,3,2,1,0:T(2,128)(2,1)} %copy.77, bf16[3,8,1,1,256]{4,3,2,1,0:T(2,128)(2,1)} %copy.68, bf16[3,1,1,8,256]{4,3,2,1,0:T(8,128)(2,1)S(1)} %bitcast.643, bf16[3,1,1,1,256]{4,3,2,1,0:T(2,128)(2,1)} %copy.76, bf16[3,1,8,1,256]{4,3,2,1,0:T(2,128)(2,1)} %copy.75, ...), kind=kLoop, calls=%fused_computation.93 | loop fusion | flops 22118400 | bytes 2611200 | tf_op jit(solution)/shard_map/concatenate | solution.py:63
  139.7 3.5 reshape.153
  143.2 3.3 fusion.75
  146.5 2.9 fusion.79
  149.4 2.9 fusion.83
  152.3 2.9 fusion.87
  155.3 2.8 fusion.91
  158.1 2.9 fusion.95
  161.0 2.9 fusion.99
  163.9 2.9 fusion.103
  166.8 2.9 fusion.107
  192.7 2.2 gather_fusion.21
  196.9 5.7 fusion.1
  202.6 3.5 reshape.155
  206.1 2.7 convolution_add_fusion.1
  208.9 2.9 convolution_add_fusion
  211.7 4.4 reshape.164
  216.2 2.7 convolution_add_fusion.3
  218.9 2.9 convolution_add_fusion.2
  221.8 4.2 reshape.163
  226.0 2.7 convolution_add_fusion.5
  228.7 2.9 convolution_add_fusion.4
  231.6 4.2 reshape.162
  235.8 2.7 convolution_add_fusion.7
  238.6 2.9 convolution_add_fusion.6
  241.4 4.2 reshape.161
  245.7 2.7 convolution_add_fusion.9
  248.4 2.9 convolution_add_fusion.8
  251.3 4.2 reshape.160
  255.5 2.7 convolution_add_fusion.11
  258.2 2.9 convolution_add_fusion.10
  261.1 4.2 reshape.159
  265.4 2.7 convolution_add_fusion.13
  268.1 2.9 convolution_add_fusion.12
  271.0 4.2 reshape.158
  275.2 2.7 convolution_add_fusion.15
  277.9 2.9 convolution_add_fusion.14
  280.8 4.2 reshape.157
  285.0 2.7 convolution_add_fusion.17
  287.8 2.9 convolution_add_fusion.16
  290.6 4.2 reshape.156
  294.8 10.5 %slice_add_fusion = bf16[3,8,8,8,256]{4,3,2,1,0:T(8,128)(2,1)} fusion(f32[3,8,10,10,256]{4,3,2,1,0:T(8,128)} %reshape.164, f32[3,8,10,10,256]{4,3,2,1,0:T(8,128)} %reshape.163, f32[3,8,10,10,256]{4,3,2,1,0:T(8,128)} %reshape.162, f32[3,8,10,10,256]{4,3,2,1,0:T(8,128)} %reshape.161, f32[3,8,10,10,256]{4,3,2,1,0:T(8,128)} %reshape.160, ...), kind=kLoop, calls=%fused_computation.112 | loop fusion | flops 3538944 | bytes 14942208 | tf_op jit(solution)/shard_map/add | solution.py:101
  305.3 2.4 reshape.165
  307.7 2.8 fusion.38
  310.5 2.3 reshape.166
  314.8 2.8 gather_fusion.26
  331.4 2.2 gather_fusion.31
  344.2 2.6 maximum_maximum_fusion
  358.8 2.9 copy-done.15
  370.2 2.2 gather_fusion.48
  381.1 7.1 %maximum_maximum_fusion.1 = bf16[3,9,10,10,256]{4,3,2,1,0:T(8,128)(2,1)S(1)} fusion(bf16[3,1,1,1,256]{4,3,2,1,0:T(2,128)(2,1)} %copy.108, bf16[3,1,1,8,256]{4,3,2,1,0:T(8,128)(2,1)} %bitcast.621, bf16[3,1,1,1,256]{4,3,2,1,0:T(2,128)(2,1)} %copy.107, bf16[3,1,8,1,256]{4,3,2,1,0:T(2,128)(2,1)} %copy.106, bf16[3,1,8,8,256]{4,3,2,1,0:T(8,128)(2,1)} %bitcast.618, ...), kind=kLoop, calls=%fused_computation.73 | loop fusion | flops 24883200 | bytes 2764800 | tf_op jit(solution)/shard_map/concatenate | solution.py:63
  399.8 2.3 fusion.186
  402.2 4.0 convolution_convert_fusion
  406.2 173.9 %all-reduce.56.cloned.1.call-done = (f32[6912,256]{1,0:T(8,128)}, f32[1024,256]{1,0:T(8,128)}) async-done(((f32[6912,256]{1,0:T(8,128)}, f32[1024,256]{1,0:T(8,128)}), (f32[6912,256]{1,0:T(8,128)}, f32[1024,256]{1,0:T(8,128)})) %all-reduce.56.cloned.1.call-update) | async-done | bytes 8126480 | tf_op jit(solution)/shard_map/psum | solution.py:172
  580.1 2.8 dynamic-slice_multiply_fusion
  (338 shorter events, 191.9 us)
Async XLA Ops:
  7.2 392.6 %copy-start = (bf16[1,24,512,128]{3,2,1,0:T(8,128)(2,1)S(1)}, bf16[1,24,512,128]{3,2,1,0:T(8,128)(2,1)}, u32[]{:S(2)}) copy-start(bf16[1,24,512,128]{3,2,1,0:T(8,128)(2,1)} %param.11) | copy-start | bytes 9437188
  7.2 9.9 %copy-start.40 = (s32[1,3,27]{2,0,1:T(1,128)S(1)}, s32[1,3,27]{2,0,1:T(1,128)}, u32[]{:S(2)}) copy-start(s32[1,3,27]{2,0,1:T(1,128)} %param.12) | copy-start | bytes 976
  7.2 572.9 %all-reduce.56.cloned.1.call-start = ((), (), s32[]{:S(2)}) async-start(), calls=%async_computation | async-start | bytes 16252928 | tf_op jit(solution)/shard_map/psum | solution.py:172
  7.2 8.4 %copy-start.16 = (bf16[1,3,512,256]{3,2,1,0:T(8,128)(2,1)S(1)}, bf16[1,3,512,256]{3,2,1,0:T(8,128)(2,1)}, u32[]{:S(2)}) copy-start(bf16[1,3,512,256]{3,2,1,0:T(8,128)(2,1)} %param.7) | copy-start | bytes 2359300
  8.4 11.6 %copy-start.18 = (bf16[1,3,512,256]{3,2,1,0:T(8,128)(2,1)S(1)}, bf16[1,3,512,256]{3,2,1,0:T(8,128)(2,1)}, u32[]{:S(2)}) copy-start(bf16[1,3,512,256]{3,2,1,0:T(8,128)(2,1)} %param.8) | copy-start | bytes 2359300
  9.7 12.7 %copy-start.14 = (bf16[1,3,512,256]{3,2,1,0:T(8,128)(2,1)}, bf16[1,3,512,256]{3,2,1,0:T(8,128)(2,1)S(1)}, u32[]{:S(2)}) copy-start(bf16[1,3,512,256]{3,2,1,0:T(8,128)(2,1)S(1)} %broadcast_maximum_fusion) | copy-start | bytes 2359300
  10.7 92.5 %collective-permute-start = (bf16[2,1,3,8,8,256]{5,4,3,2,1,0:T(8,128)(2,1)}, bf16[2,1,3,8,8,256]{5,4,3,2,1,0:T(8,128)(2,1)}, u32[]{:S(2)}, u32[]{:S(2)}) collective-permute-start(bf16[2,1,3,8,8,256]{5,4,3,2,1,0:T(8,128)(2,1)} %get-tuple-element.57), channel_id=1, source_target_pairs={{1,0},{2,1},{3,2},{4,3},{5,4},{6,5},{7,6},{9,8},{10,9},{11,10},{12... | collective-permute-start | bytes 589832 | tf_op jit(solution)/shard_map/ppermute | solution.py:19
  11.9 95.3 %collective-permute-start.1 = (bf16[2,1,3,8,8,256]{5,4,3,2,1,0:T(8,128)(2,1)}, bf16[2,1,3,8,8,256]{5,4,3,2,1,0:T(8,128)(2,1)}, u32[]{:S(2)}, u32[]{:S(2)}) collective-permute-start(bf16[2,1,3,8,8,256]{5,4,3,2,1,0:T(8,128)(2,1)} %get-tuple-element.56), channel_id=1, source_target_pairs={{0,1},{1,2},{2,3},{3,4},{4,5},{5,6},{6,7},{8,9},{9,10},{10,11},{11... | collective-permute-start | bytes 589832 | tf_op jit(solution)/shard_map/ppermute | solution.py:16
  36.3 1.2 copy-start.34
  38.5 20.5 %copy-start.20 = (bf16[3,8,8,1,256]{4,3,2,1,0:T(2,128)(2,1)}, bf16[3,8,8,1,256]{4,3,2,1,0:T(2,128)(2,1)S(1)}, u32[]{:S(2)}) copy-start(bf16[3,8,8,1,256]{4,3,2,1,0:T(2,128)(2,1)S(1)} %copy.66) | copy-start | bytes 294916
  48.3 18.0 %copy-start.21 = (bf16[3,8,8,1,256]{4,3,2,1,0:T(2,128)(2,1)}, bf16[3,8,8,1,256]{4,3,2,1,0:T(2,128)(2,1)S(1)}, u32[]{:S(2)}) copy-start(bf16[3,8,8,1,256]{4,3,2,1,0:T(2,128)(2,1)S(1)} %copy.65) | copy-start | bytes 294916
  62.7 12.9 %copy-start.28 = (bf16[3,8,8,1,256]{4,3,2,1,0:T(2,128)(2,1)S(1)}, bf16[3,8,8,1,256]{4,3,2,1,0:T(2,128)(2,1)}, u32[]{:S(2)}) copy-start(bf16[3,8,8,1,256]{4,3,2,1,0:T(2,128)(2,1)} %get-tuple-element.40) | copy-start | bytes 294916
  88.1 13.8 %copy-start.29 = (bf16[3,8,1,1,256]{4,3,2,1,0:T(2,128)(2,1)}, bf16[3,8,1,1,256]{4,3,2,1,0:T(2,128)(2,1)S(1)}, u32[]{:S(2)}) copy-start(bf16[3,8,1,1,256]{4,3,2,1,0:T(2,128)(2,1)S(1)} %copy.93) | copy-start | bytes 36868
  97.0 4.9 copy-start.37
  97.0 5.0 copy-start.38
  97.0 5.6 copy-start.35
  97.0 5.6 copy-start.36
  143.2 3.3 copy-start.10
  166.8 2.9 copy-start.27
  166.8 5.4 copy-start.26
  166.8 8.0 %copy-start.33 = (bf16[3,1,1,1,256]{4,3,2,0,1:T(2,128)(2,1)S(1)}, bf16[3,1,1,1,256]{4,3,2,0,1:T(2,128)(2,1)}, u32[]{:S(2)}) copy-start(bf16[3,1,1,1,256]{4,3,2,0,1:T(2,128)(2,1)} %get-tuple-element.79) | copy-start | bytes 4612
  166.8 10.5 %copy-start.30 = (bf16[3,1,1,8,256]{4,3,2,0,1:T(8,128)(2,1)S(1)}, bf16[3,1,1,8,256]{4,3,2,0,1:T(8,128)(2,1)}, u32[]{:S(2)}) copy-start(bf16[3,1,1,8,256]{4,3,2,0,1:T(8,128)(2,1)} %get-tuple-element.83) | copy-start | bytes 36868
  206.1 2.7 copy-start.1
  216.1 2.8 copy-start.2
  226.0 2.8 copy-start.3
  235.8 2.8 copy-start.4
  245.7 2.7 copy-start.5
  255.5 2.8 copy-start.6
  265.4 2.7 copy-start.7
  275.2 2.7 copy-start.8
  285.0 2.7 copy-start.9
  312.7 10.2 %copy-start.32 = (bf16[3,1,1,1,256]{4,3,2,0,1:T(2,128)(2,1)S(1)}, bf16[3,1,1,1,256]{4,3,2,0,1:T(2,128)(2,1)}, u32[]{:S(2)}) copy-start(bf16[3,1,1,1,256]{4,3,2,0,1:T(2,128)(2,1)} %get-tuple-element.71) | copy-start | bytes 4612
  319.6 79.0 %collective-permute-start.3 = (bf16[8,64,256]{2,1,0:T(8,128)(2,1)}, bf16[8,64,256]{2,1,0:T(8,128)(2,1)}, u32[]{:S(2)}, u32[]{:S(2)}) collective-permute-start(bf16[8,64,256]{2,1,0:T(8,128)(2,1)} %get-tuple-element.43), channel_id=1, source_target_pairs={{0,1},{1,2},{2,3},{3,4},{4,5},{5,6},{6,7},{7,0},{8,9},{9,10},{10,1... | collective-permute-start | bytes 786440 | tf_op jit(solution)/shard_map/ppermute | solution.py:27
  321.5 77.2 %collective-permute-start.2 = (bf16[8,64,256]{2,1,0:T(8,128)(2,1)}, bf16[8,64,256]{2,1,0:T(8,128)(2,1)}, u32[]{:S(2)}, u32[]{:S(2)}) collective-permute-start(bf16[8,64,256]{2,1,0:T(8,128)(2,1)} %get-tuple-element.41), channel_id=1, source_target_pairs={{0,7},{1,0},{2,1},{3,2},{4,3},{5,4},{6,5},{7,6},{8,15},{9,8},{10,9... | collective-permute-start | bytes 786440 | tf_op jit(solution)/shard_map/ppermute | solution.py:27
  342.3 4.5 copy-start.11
  350.5 1.5 copy-start.24
  352.9 1.1 copy-start.13
  354.0 1.1 copy-start.17
  354.0 1.4 copy-start.19
  354.0 1.4 copy-start.39
  355.9 1.5 copy-start.23
  358.3 3.4 copy-start.31
  358.8 2.9 copy-start.15
  381.1 7.1 %copy-start.12 = (bf16[3,8,8,8,256]{4,3,2,1,0:T(8,128)(2,1)S(1)}, bf16[3,8,8,8,256]{4,3,2,1,0:T(8,128)(2,1)}, u32[]{:S(2)}) copy-start(bf16[3,8,8,8,256]{4,3,2,1,0:T(8,128)(2,1)} %get-tuple-element.95) | copy-start | bytes 2359300
  397.5 1.2 copy-start.25
  399.8 2.4 copy-start.22
Sparse Core Ops, SparseCore 0:
  402.3 177.6 all-reduce.55
where the time goes:
time: 600 us; the launch traced here: 592 us
  local copies, waits for them, and re-layouts  214 us (36%)
  waiting for transfers between devices  174 us (29%)
  matrix products  102 us (17%)
  other arithmetic  77.9 us (13%)
  between operations  15 us (2%)
  starting transfers between devices  8.3 us (1%)
    psum x1, waiting for transfers between devices, body(): conv_sum, down_sum = lax.psum((conv_part, down_part), ('dp', 'dom'))  174 us
    gather x89, local copies, waits for them, and re-layouts, pick_rows(): return extended[jnp.where(slot_index < 0, source.shape[0], slot_index)]  97.9 us
    dot_general x27, matrix products, correlate(): lax.dot_general(slabs[index_x], weight[position], (((1,), (1,)), ((), ())...  76.8 us
    reshape x9, local copies, waits for them, and re-layouts, correlate(): plane_sum.reshape(count_blocks, block_edge, span, span, weight.shape[1])  38.1 us
    unnamed x155, local copies, waits for them, and re-layouts  26.8 us
    concatenate x4, other arithmetic, assemble(): return jnp.concatenate(parts_x, axis=1)  21.7 us
    dot_general x27, matrix products, correlate(): lax.dot_general(window(act_pad, 1 + tap_x, 1 + tap_y, 1 + tap_z), centre_...  19 us
    gather x14, other arithmetic, pick_rows(): return extended[jnp.where(slot_index < 0, source.shape[0], slot_index)]  16.3 us
  transfers between devices with their start and end apart: 5, of which 1 were waited for; matrix products, arithmetic and copies ran while one was open for 28% of the time, Pallas kernels for 0%

commit v1 on v0

v1 whole, which is shorter than its diff:
```python
import functools
import math

import jax
import jax.numpy as jnp
from jax import lax
from jax.experimental import pallas as pl
from jax.experimental.pallas import tpu as pltpu
from jax.sharding import PartitionSpec as P

BE = 8
PLANE = BE * BE
HALF = BE // 2
F32 = jnp.float32
BF16 = jnp.bfloat16
MIB = 1 << 20

VMEM = pl.BlockSpec(memory_space=pltpu.VMEM)
SMEM = pl.BlockSpec(memory_space=pltpu.SMEM)
ANY = pl.BlockSpec(memory_space=pl.ANY)


def params(mib):
    return pltpu.CompilerParams(vmem_limit_bytes=mib * MIB)


def relative(index, step, count):
    if count & (count - 1) == 0:
        return index ^ step
    return lax.rem(index + step, count)


def source_of(index, step, count):
    if count & (count - 1) == 0:
        return index ^ step
    return (index - step) % count if isinstance(index, int) else lax.rem(index + count - step, count)


def exchange(value, axis, step, stride):
    count = lax.axis_size(axis) // stride
    pairs = []
    for index in range(lax.axis_size(axis)):
        high, low = divmod(index, stride)
        other = high ^ step if count & (count - 1) == 0 else (high + step) % count
        pairs.append((index, other * stride + low))
    return lax.ppermute(value, axis, pairs)


def fetch(ref, slot, start, rows):
    value = ref[jnp.maximum(slot, 0), pl.ds(start, rows), :].astype(F32)
    return jnp.where(slot >= 0, value, 0.0)


def spread(links_ref, ref, start, step_x, slot, row, win_ref):
    channels = ref.shape[-1]

    def link(step_y, step_z):
        return links_ref[slot, 9 * (step_x + 1) + 3 * (step_y + 1) + step_z + 1]

    columns = {}
    for step_z in (-1, 0, 1):
        below = fetch(ref, link(-1, step_z), start + PLANE - 16, 16).reshape(2, BE, channels)[1:]
        middle = fetch(ref, link(0, step_z), start, PLANE).reshape(BE, BE, channels)
        above = fetch(ref, link(1, step_z), start, 16).reshape(2, BE, channels)[:1]
        columns[step_z] = jnp.concatenate([below, middle, above], axis=0)
    place_z = lax.broadcasted_iota(jnp.int32, columns[0].shape, 1)
    shifted = {
        0: columns[0],
        -1: jnp.where(
            place_z == 0, pltpu.roll(columns[-1], 1, axis=1), pltpu.roll(columns[0], 1, axis=1)
        ),
        1: jnp.where(
            place_z == BE - 1,
            pltpu.roll(columns[1], BE - 1, axis=1),
            pltpu.roll(columns[0], BE - 1, axis=1),
        ),
    }
    for tap_y in (-1, 0, 1):
        for tap_z in (-1, 0, 1):
            tap = 3 * (tap_y + 1) + tap_z + 1
            value = shifted[-tap_z][1 - tap_y : 1 - tap_y + BE].reshape(PLANE, channels)
            win_ref[pl.ds(row, PLANE), tap * channels : (tap + 1) * channels] = value.astype(BF16)


def build_windows(links_ref, own_ref, low_ref, high_ref, win_ref):
    slots = own_ref.shape[0]

    def edge(slot, carry):
        spread(links_ref, low_ref, 0, -1, slot, pl.multiple_of(slot * PLANE, PLANE), win_ref)
        row = ((BE + 1) * slots + slot) * PLANE
        spread(links_ref, high_ref, 0, 1, slot, pl.multiple_of(row, PLANE), win_ref)
        return carry

    def inner(step, carry):
        x = step // slots
        slot = step - x * slots
        row = (x + 1) * slots * PLANE + slot * PLANE
        start = pl.multiple_of(x * PLANE, PLANE)
        spread(links_ref, own_ref, start, 0, slot, pl.multiple_of(row, PLANE), win_ref)
        return carry

    lax.fori_loop(0, slots, edge, 0)
    lax.fori_loop(0, BE * slots, inner, 0)


def input_kernel(
    links_ref, routes_ref, own_ref, low_ref, high_ref, pre_ref, weight_ref,
    to_lower_ref, stay_ref, to_upper_ref,
    win_ref, taps_ref, acc_ref, octants_ref, tap_sems, out_sems,
):
    slots, voxels, channels = own_ref.shape
    places = routes_ref.shape[1]
    groups = places // 8
    copies = []
    for tap in range(27):
        index_x, rest = divmod(tap, 9)
        copy = pltpu.make_async_copy(
            weight_ref.at[tap],
            taps_ref.at[index_x, :, rest * channels : (rest + 1) * channels],
            tap_sems.at[tap],
        )
        copy.start()
        copies.append(copy)
    build_windows(links_ref, own_ref, low_ref, high_ref, win_ref)
    for copy in copies:
        copy.wait()
    slab = slots * PLANE
    rows = BE * slab
    half = rows // 2

    def multiply(part, carry):
        start = part * half
        total = None
        for index_x in range(3):
            offset = pl.multiple_of(start + (2 - index_x) * slab, PLANE)
            term = lax.dot_general(
                win_ref[pl.ds(offset, half), :],
                taps_ref[index_x],
                (((1,), (1,)), ((), ())),
                preferred_element_type=F32,
            )
            total = term if total is None else total + term
        acc_ref[pl.ds(pl.multiple_of(start, PLANE), half), :] = total
        return carry

    lax.fori_loop(0, 2, multiply, 0)
    octants_ref[...] = jnp.zeros_like(octants_ref)
    place_z = lax.broadcasted_iota(jnp.int32, (BE // 2, BE, channels), 1)
    for slot in range(slots):
        group = jnp.int32(3 * groups)
        for row in range(3):
            for part in range(groups):
                group = jnp.where(
                    routes_ref[row, 8 * part] == 8 * slot, row * groups + part, group
                )

        def finish(x, carry):
            value = acc_ref[pl.ds(pl.multiple_of(x * slab + slot * PLANE, PLANE), PLANE), :]
            pre = pre_ref[slot, pl.ds(pl.multiple_of(x * PLANE, PLANE), PLANE), :].astype(F32)
            value = jnp.where(pre > 0, value, 0.0).reshape(BE // 2, 2, BE, channels)
            even, odd = value[:, 0], value[:, 1]
            near = jnp.where(place_z < HALF, even, pltpu.roll(odd, HALF, axis=1))
            far = jnp.where(place_z < HALF, pltpu.roll(even, HALF, axis=1), odd)
            side = x // HALF
            row = (x - side * HALF) * 16
            for side_y in range(2):
                for side_z, piece in enumerate((near, far)):
                    block = piece[2 * side_y : 2 * side_y + 2].reshape(16, channels).astype(BF16)
                    start = (4 * side + 2 * side_y + side_z) * PLANE + row
                    octants_ref[group, pl.ds(pl.multiple_of(start, 16), 16), :] = block
            return carry

        lax.fori_loop(0, BE, finish, 0)
    outs = []
    for row, ref in enumerate((to_lower_ref, stay_ref, to_upper_ref)):
        copy = pltpu.make_async_copy(
            octants_ref.at[pl.ds(row * groups, groups)], ref, out_sems.at[row]
        )
        copy.start()
        outs.append(copy)
    for copy in outs:
        copy.wait()


def input_gradient(links, routes, own, low, high, pre, weight):
    slots, voxels, channels = own.shape
    groups = routes.shape[1] // 8
    rows = slots * voxels
    out = jax.ShapeDtypeStruct((groups, voxels, channels), BF16)
    return pl.pallas_call(
        input_kernel,
        out_shape=(out, out, out),
        in_specs=[SMEM, SMEM, VMEM, VMEM, VMEM, VMEM, ANY],
        out_specs=(ANY, ANY, ANY),
        scratch_shapes=[
            pltpu.VMEM((slots * PLANE * (BE + 2), 9 * channels), BF16),
            pltpu.VMEM((3, channels, 9 * channels), BF16),
            pltpu.VMEM((rows, channels), F32),
            pltpu.VMEM((3 * groups + 1, voxels, channels), BF16),
            pltpu.SemaphoreType.DMA((27,)),
            pltpu.SemaphoreType.DMA((3,)),
        ],
        compiler_params=params(48),
        cost_estimate=pl.CostEstimate(
            flops=2 * rows * 27 * channels * channels, bytes_accessed=8 * MIB, transcendentals=0
        ),
        name="input_gradient",
    )(links, routes, own, low, high, pre, weight)


def filter_kernel(
    shard_rows, where_ref, links_ref, own_ref, low_ref, high_ref, pre_ref,
    keep_ref, send_ref, win_ref, act_ref,
):
    slots, voxels, channels = own_ref.shape
    slab = slots * PLANE
    rows = BE * slab
    lanes = channels // 2
    for pair in range(BE // 2):
        parts = []
        for x in (2 * pair, 2 * pair + 1):
            for slot in range(slots):
                parts.append(pre_ref[slot, x * PLANE : (x + 1) * PLANE, :])
        block = jnp.maximum(jnp.concatenate(parts, axis=0).astype(F32), 0.0)
        act_ref[:, pair * 2 * slab : (pair + 1) * 2 * slab] = block.T.astype(BF16)
    build_windows(links_ref, own_ref, low_ref, high_ref, win_ref)
    first = lax.rem(where_ref[0], 2) == 0
    unit = math.gcd(channels, shard_rows)

    def step(index_x, carry):
        offset = pl.multiple_of((2 - index_x) * slab, PLANE)
        for rest in range(9):
            total = jnp.dot(
                act_ref[...],
                win_ref[pl.ds(offset, rows), rest * channels : (rest + 1) * channels],
                preferred_element_type=F32,
            )
            left, right = total[:, :lanes], total[:, lanes:]
            keep = jnp.where(first, left, right).astype(BF16)
            send = jnp.where(first, right, left).astype(BF16)
            for part in range(channels // unit):
                row = (index_x * 9 + rest) * channels + part * unit
                shard = row // shard_rows
                start = pl.multiple_of(row - shard * shard_rows, unit)
                span = slice(part * unit, (part + 1) * unit)
                keep_ref[shard, pl.ds(start, unit), :] = keep[span]
                send_ref[shard, pl.ds(start, unit), :] = send[span]
        return carry

    lax.fori_loop(0, 3, step, 0)


def filter_gradient(shards, where, links, own, low, high, pre):
    slots, voxels, channels = own.shape
    shard_rows = 27 * channels // shards
    rows = slots * voxels
    out = jax.ShapeDtypeStruct((shards, shard_rows, channels // 2), BF16)
    return pl.pallas_call(
        functools.partial(filter_kernel, shard_rows),
        out_shape=(out, out),
        in_specs=[SMEM, SMEM, VMEM, VMEM, VMEM, VMEM],
        out_specs=(VMEM, VMEM),
        scratch_shapes=[
            pltpu.VMEM((slots * PLANE * (BE + 2), 9 * channels), BF16),
            pltpu.VMEM((channels, rows), BF16),
        ],
        compiler_params=params(48),
        cost_estimate=pl.CostEstimate(
            flops=2 * rows * 27 * channels * channels, bytes_accessed=8 * MIB, transcendentals=0
        ),
        name="filter_gradient",
    )(where, links, own, low, high, pre)


def fine_kernel(
    where_ref, upper_ref, stay_ref, lower_ref, weight_ref, act_ref,
    grad_ref, keep_ref, send_ref, acc_ref,
):
    step = pl.program_id(0)
    fine, voxels, fine_channels = act_ref.shape
    channels = upper_ref.shape[-1]
    taps = weight_ref.shape[0]
    cells = voxels // taps

    @pl.when(step == 0)
    def _():
        acc_ref[...] = jnp.zeros_like(acc_ref)

    def work(ref):
        octants = ref[0]
        product = lax.dot_general(
            octants,
            weight_ref[...].reshape(taps * fine_channels, channels),
            (((1,), (1,)), ((), ())),
            preferred_element_type=F32,
        ).astype(BF16)
        wide = []
        for place in range(fine):
            for tap in range(taps):
                grad_ref[place, tap * cells : (tap + 1) * cells, :] = product[
                    place * cells : (place + 1) * cells,
                    tap * fine_channels : (tap + 1) * fine_channels,
                ]
            wide.append(
                jnp.concatenate(
                    [act_ref[place, tap * cells : (tap + 1) * cells, :] for tap in range(taps)],
                    axis=1,
                )
            )
        acc_ref[...] += jnp.dot(
            octants.T, jnp.concatenate(wide, axis=0), preferred_element_type=F32
        )

    for row, ref in enumerate((upper_ref, stay_ref, lower_ref)):
        pl.when(step == row)(functools.partial(work, ref))

    @pl.when(step == pl.num_programs(0) - 1)
    def _():
        first = lax.rem(where_ref[0], 2) == 0
        total = acc_ref[...].T
        lanes = channels // 2
        left, right = total[:, :lanes], total[:, lanes:]
        keep_ref[...] = jnp.where(first, left, right).astype(BF16).reshape(keep_ref.shape)
        send_ref[...] = jnp.where(first, right, left).astype(BF16).reshape(send_ref.shape)


def fine_gradient(shards, where, from_upper, stay, from_lower, weight, fine_act):
    fine, voxels, fine_channels = fine_act.shape
    groups, _, channels = stay.shape
    taps = weight.shape[0]
    per_row = 8
    whole = pl.BlockSpec((1, voxels, channels), lambda i: (0, 0, 0))
    out = jax.ShapeDtypeStruct((shards, taps * fine_channels // shards, channels // 2), BF16)
    same = pl.BlockSpec(out.shape, lambda i: (0, 0, 0))
    block = pl.BlockSpec((per_row, voxels, fine_channels), lambda i: (i, 0, 0))
    return pl.pallas_call(
        fine_kernel,
        grid=(3,),
        out_shape=(jax.ShapeDtypeStruct(fine_act.shape, BF16), out, out),
        in_specs=[
            SMEM, whole, whole, whole,
            pl.BlockSpec(weight.shape, lambda i: (0, 0, 0)),
            block,
        ],
        out_specs=(block, same, same),
        scratch_shapes=[pltpu.VMEM((channels, taps * fine_channels), F32)],
        compiler_params=params(40),
        cost_estimate=pl.CostEstimate(
            flops=4 * fine * voxels * fine_channels * channels, bytes_accessed=8 * MIB,
            transcendentals=0,
        ),
        name="fine_gradient",
    )(where, from_upper, stay, from_lower, weight, fine_act)


def pair_kernel(count, piece, where_ref, *refs):
    keeps, gots, outs = refs[:2], refs[2:4], refs[4 : 4 + count]
    scratch = refs[4 + count]
    shards = scratch.shape[0]
    start = 0
    for keep_ref, got_ref in zip(keeps, gots):
        rows = keep_ref.shape[1]
        scratch[:, start : start + rows, :] = keep_ref[...].astype(F32) + got_ref[...].astype(F32)
        start += rows
    high = where_ref[0] // 2
    for step, ref in enumerate(outs):
        row = pl.multiple_of(relative(high, step, count) * piece, 16)
        ref[...] = scratch[:, pl.ds(row, piece), :].astype(ref.dtype)


def pair_sum(where, count, piece, keeps, gots):
    shards, _, lanes = keeps[0].shape
    shape = (shards, piece, lanes)
    return pl.pallas_call(
        functools.partial(pair_kernel, count, piece),
        out_shape=[jax.ShapeDtypeStruct(shape, F32 if step == 0 else BF16) for step in range(count)],
        in_specs=[SMEM] + [VMEM] * 4,
        out_specs=[VMEM] * count,
        scratch_shapes=[pltpu.VMEM((shards, piece * count, lanes), F32)],
        compiler_params=params(40),
        name="pair_sum",
    )(where, *keeps, *gots)


def plane_kernel(count, where_ref, *refs):
    shards = refs[0].shape[0]
    outs = refs[count:]
    for step, ref in enumerate(outs):
        shard = relative(where_ref[1], step, shards)
        total = refs[0][shard].astype(F32)
        for part in refs[1:count]:
            total = total + part[shard].astype(F32)
        ref[...] = total.astype(ref.dtype)


def plane_sum(where, parts):
    shards, piece, lanes = parts[0].shape
    return pl.pallas_call(
        functools.partial(plane_kernel, len(parts)),
        out_shape=[
            jax.ShapeDtypeStruct((piece, lanes), F32 if step == 0 else BF16)
            for step in range(shards)
        ],
        in_specs=[SMEM] + [VMEM] * len(parts),
        out_specs=[VMEM] * shards,
        compiler_params=params(40),
        name="plane_sum",
    )(where, *parts)


def slab_kernel(factor, *refs):
    total = refs[0][...]
    for part in refs[1:-1]:
        total = total + part[...].astype(F32)
    refs[-1][...] = (total * factor).astype(BF16)


def slab_sum(factor, parts):
    return pl.pallas_call(
        functools.partial(slab_kernel, factor),
        out_shape=jax.ShapeDtypeStruct(parts[0].shape, BF16),
        in_specs=[VMEM] * len(parts),
        out_specs=VMEM,
        compiler_params=params(40),
        name="slab_sum",
    )(*parts)


def gather_kernel(count, where_ref, *refs):
    near, far = refs[:count], refs[count : 2 * count]
    conv_ref, down_ref, scratch = refs[2 * count :]
    piece, lanes = near[0].shape
    high = where_ref[0] // 2
    low = lax.rem(where_ref[0], 2)
    for side, parts in ((low, near), (1 - low, far)):
        lane = pl.multiple_of(side * lanes, lanes)
        for step, ref in enumerate(parts):
            row = pl.multiple_of(source_of(high, step, count) * piece, 16)
            scratch[pl.ds(row, piece), pl.ds(lane, lanes)] = ref[...].astype(F32)
    conv_rows = conv_ref.shape[0]
    conv_ref[...] = scratch[:conv_rows]
    down_ref[...] = scratch[conv_rows : conv_rows + down_ref.shape[0]]


def gather_up(where, conv_rows, down_rows, near, far):
    piece, lanes = near[0].shape
    count = len(near)
    return pl.pallas_call(
        functools.partial(gather_kernel, count),
        out_shape=(
            jax.ShapeDtypeStruct((conv_rows, 2 * lanes), F32),
            jax.ShapeDtypeStruct((down_rows, 2 * lanes), F32),
        ),
        in_specs=[SMEM] + [VMEM] * (2 * count),
        out_specs=(VMEM, VMEM),
        scratch_shapes=[pltpu.VMEM((count * piece, 2 * lanes), F32)],
        compiler_params=params(40),
        name="gather_up",
    )(where, *near, *far)


def body(grad_out, pre_act, conv_weight, down_weight, fine_act, neighbours, octant_routes):
    own = grad_out[0]
    pre = pre_act[0]
    links = neighbours[0]
    routes = octant_routes[0, 0]
    slots, voxels, channels = own.shape
    devices = lax.axis_size("dom")
    shards = lax.axis_size("dp")
    where = jnp.stack([lax.axis_index("dom"), lax.axis_index("dp")]).astype(jnp.int32)

    forward = [(i, i + 1) for i in range(devices - 1)]
    backward = [(i + 1, i) for i in range(devices - 1)]
    low = lax.ppermute(own[:, voxels - PLANE :], "dom", forward)
    high = lax.ppermute(own[:, :PLANE], "dom", backward)

    to_lower, stay, to_upper = input_gradient(links, routes, own, low, high, pre, conv_weight)
    ring = [(i, (i + 1) % devices) for i in range(devices)]
    from_upper = lax.ppermute(to_lower, "dom", [(b, a) for a, b in ring])
    from_lower = lax.ppermute(to_upper, "dom", ring)
    conv_keep, conv_send = filter_gradient(shards, where, links, own, low, high, pre)
    fine_grad, down_keep, down_send = fine_gradient(
        shards, where, from_upper, stay, from_lower, down_weight, fine_act[0]
    )

    count = devices // 2
    conv_rows, down_rows = conv_keep.shape[1], down_keep.shape[1]
    piece = -(-(conv_rows + down_rows) // (16 * count)) * 16
    swap = [(i, i ^ 1) for i in range(devices)]
    conv_got = lax.ppermute(conv_send, "dom", swap)
    down_got = lax.ppermute(down_send, "dom", swap)
    parts = pair_sum(where, count, piece, (conv_keep, down_keep), (conv_got, down_got))
    parts = [parts[0]] + [exchange(parts[step], "dom", step, 2) for step in range(1, count)]
    parts = plane_sum(where, parts)
    parts = [parts[0]] + [exchange(parts[step], "dp", step, 1) for step in range(1, shards)]
    factor = 1.0 / math.sqrt(shards * devices * slots * voxels)
    mine = slab_sum(factor, parts)
    near = [mine] + [exchange(mine, "dom", step, 2) for step in range(1, count)]
    far = [lax.ppermute(value, "dom", swap) for value in near]
    conv_grad, down_grad = gather_up(where, conv_rows, down_rows, near, far)
    return (fine_grad[None], conv_grad, down_grad)


def solution(mesh):
    return jax.shard_map(
        body,
        mesh=mesh,
        in_specs=(
            P("dp", "dom", None, None),
            P("dp", "dom", None, None),
            P(),
            P(),
            P("dp", "dom", None, None),
            P("dp", "dom", None),
            P("dp", "dom", None, None),
        ),
        out_specs=(P("dp", "dom", None, None), P("dp", None), P("dp", None)),
        check_vma=False,
    )
```

time: 600 us -> 101 us (0.17); the launches traced: 592 us -> 101 us
  local copies, waits for them, and re-layouts: 214 us -> 3.94 us
  waiting for transfers between devices: 174 us -> 47.1 us
  matrix products: 102 us -> 0 us
  other arithmetic: 77.9 us -> 0.07 us
  Pallas kernels: 0 us -> 26.6 us
  starting transfers between devices: 8.3 us -> 22.6 us
  between operations: 15 us -> 0.75 us
    psum x1 -> x0, waiting for transfers between devices: 174 us -> none  [body(): conv_sum, down_sum = lax.psum((conv_part, down_part), ('dp', 'dom'))]
    dot_general x56 -> x0, matrix products: 102 us -> none  [the longest x27 76.8 us: correlate(): lax.dot_general(slabs[index_x], weight[position], (((1,), (1,)), ((), ())...]
    gather x89 -> x0, local copies, waits for them, and re-layouts: 97.9 us -> none  [pick_rows(): return extended[jnp.where(slot_index < 0, source.shape[0], slot_index)]]
    reshape x14 -> x0, local copies, waits for them, and re-layouts: 53.5 us -> none  [the longest x9 38.1 us: correlate(): plane_sum.reshape(count_blocks, block_edge, span, span, weight.shape[1])]
    ppermute x4 -> x19, waiting for transfers between devices: 0.01 us -> 47.1 us  [the longest x9 34.6 us: exchange(): return lax.ppermute(value, axis, pairs)]
    concatenate x8 -> x0, other arithmetic: 32.2 us -> none  [the longest x4 21.7 us: assemble(): return jnp.concatenate(parts_x, axis=1)]
    pallas_call x0 -> x7, Pallas kernels: none -> 26.6 us  [the longest x1 9.46 us: input_gradient(): pl.pallas_call(input_kernel, out_shape=(out, out, out), in_specs=[SMEM, S...]
    unnamed x155 -> x18, local copies, waits for them, and re-layouts: 26.8 us -> 2.98 us
  transfers between devices with their start and end apart: 5 -> 19, of which waited for: 1 -> 13; matrix products, arithmetic and copies ran while one was open for 28% -> 1% of each run, Pallas kernels for 0% -> 13%
where the time goes in v1:
time: 101 us
  waiting for transfers between devices  47.1 us (47%)
  Pallas kernels  26.6 us (26%)
  starting transfers between devices  22.6 us (22%)
  local copies, waits for them, and re-layouts  3.94 us (4%)
    ppermute x9, waiting for transfers between devices, exchange(): return lax.ppermute(value, axis, pairs)  34.6 us
    ppermute x9, starting transfers between devices, exchange(): return lax.ppermute(value, axis, pairs)  11.6 us
    pallas_call x1, Pallas kernels, input_gradient(): pl.pallas_call(input_kernel, out_shape=(out, out, out), in_specs=[SMEM, S...  9.46 us
    pallas_call x1, Pallas kernels, filter_gradient(): pl.pallas_call(functools.partial(filter_kernel, shard_rows), out_shape=(o...  8.65 us
    ppermute x1, waiting for transfers between devices, body(): from_upper = lax.ppermute(to_lower, 'dom', [(b, a) for a, b in ring])  5.18 us
    ppermute x1, waiting for transfers between devices, body(): from_lower = lax.ppermute(to_upper, 'dom', ring)  4.26 us
    pallas_call x1, Pallas kernels, fine_gradient(): pl.pallas_call(fine_kernel, grid=(3,), out_shape=(jax.ShapeDtypeStruct(fi...  4.1 us
    ppermute x1, starting transfers between devices, body(): from_upper = lax.ppermute(to_lower, 'dom', [(b, a) for a, b in ring])  3.41 us
  transfers between devices with their start and end apart: 19, of which 13 were waited for; matrix products, arithmetic and copies ran while one was open for 1% of the time, Pallas kernels for 13%

profile of v1, /device:TPU:0, one launch (start us, length us, event | category | flops | bytes accessed | tf_op | source)
XLA Modules:
  0.0 101.0 jit_solution(18325835097910463924)
XLA Ops:
  0.6 1.0 fusion
  1.6 1.3 %collective-permute-start.1 = (bf16[3,64,256]{2,1,0:T(8,128)(2,1)S(1)}, bf16[3,64,256]{2,1,0:T(8,128)(2,1)S(1)}, u32[]{:S(2)}, u32[]{:S(2)}) collective-permute-start(bf16[3,64,256]{2,1,0:T(8,128)(2,1)S(1)} %get-tuple-element.39), channel_id=1, source_target_pairs={{1,0},{2,1},{3,2},{4,3},{5,4},{6,5},{7,6},{9,8},{10,9},{11,10},{12... | collective-permute-start | bytes 294920 | tf_op jit(solution)/shard_map/ppermute | solution.py:475
  2.9 3.0 %collective-permute-start = (bf16[3,64,256]{2,1,0:T(8,128)(2,1)S(1)}, bf16[3,64,256]{2,1,0:T(8,128)(2,1)S(1)}, u32[]{:S(2)}, u32[]{:S(2)}) collective-permute-start(bf16[3,64,256]{2,1,0:T(8,128)(2,1)S(1)} %get-tuple-element.40), channel_id=1, source_target_pairs={{0,1},{1,2},{2,3},{3,4},{4,5},{5,6},{6,7},{8,9},{9,10},{10,11},{11... | collective-permute-start | bytes 294920 | tf_op jit(solution)/shard_map/ppermute | solution.py:474
  5.9 0.7 copy.15
  6.6 0.1 pad_add_fusion.where_ref
  6.7 0.0 collective-permute-done.1.high_ref
  6.7 0.2 collective-permute-done.low_ref
  6.9 0.0 copy-start
  6.9 1.1 %copy-done = bf16[1,3,512,256]{3,2,1,0:T(8,128)(2,1)S(1)} copy-done((bf16[1,3,512,256]{3,2,1,0:T(8,128)(2,1)S(1)}, bf16[1,3,512,256]{3,2,1,0:T(8,128)(2,1)}, u32[]{:S(2)}) %copy-start) | copy-done | bytes 786456
  8.0 0.0 copy-start.4
  8.0 1.1 %copy-done.4 = bf16[1,3,512,256]{3,2,1,0:T(8,128)(2,1)S(1)} copy-done((bf16[1,3,512,256]{3,2,1,0:T(8,128)(2,1)S(1)}, bf16[1,3,512,256]{3,2,1,0:T(8,128)(2,1)}, u32[]{:S(2)}) %copy-start.4) | copy-done | bytes 786456
  9.1 0.0 copy-start.7
  9.1 0.0 copy-start.1
  9.1 0.0 copy-start.2
  9.1 0.0 copy-start.5
  9.1 8.6 %filter_gradient.1 = (bf16[4,1728,128]{2,1,0:T(8,128)(2,1)S(1)}, bf16[4,1728,128]{2,1,0:T(8,128)(2,1)S(1)}) custom-call(s32[2]{0:T(128)S(1)} %pad_add_fusion.where_ref, s32[3,27]{1,0:T(4,128)S(1)} %bitcast.15, bf16[3,512,256]{2,1,0:T(8,128)(2,1)S(1)} %bitcast.13, bf16[3,64,256]{2,1,0:T(8,128)(2,1)S(1)} %collective-permute-done.low_ref, ...), custom_call_target="tpu_custom_call" | custom-call | flops 5435817984 | bytes 8388608 | tf_op jit(solution)/shard_map/filter_gradient/pallas_call | solution.py:258
  17.8 3.3 %collective-permute-start.4 = (bf16[4,1728,128]{2,1,0:T(8,128)(2,1)S(1)}, bf16[4,1728,128]{2,1,0:T(8,128)(2,1)S(1)}, u32[]{:S(2)}, u32[]{:S(2)}) collective-permute-start(bf16[4,1728,128]{2,1,0:T(8,128)(2,1)S(1)} %get-tuple-element.27), channel_id=1, source_target_pairs={{0,1},{1,0},{2,3},{3,2},{4,5},{5,4},{6,7},{7,6},{8,9},{9,8},{10,11... | collective-permute-start | bytes 5308424 | tf_op jit(solution)/shard_map/ppermute | solution.py:490
  21.1 0.0 copy-done.7
  21.1 0.0 copy-done.1
  21.1 0.0 copy-done.2
  21.1 0.0 copy-done.5
  21.1 0.0 copy-start.3
  21.1 0.0 copy-start.6
  21.2 9.5 %input_gradient.1 = (bf16[1,512,256]{2,1,0:T(8,128)(2,1)S(1)}, bf16[1,512,256]{2,1,0:T(8,128)(2,1)S(1)}, bf16[1,512,256]{2,1,0:T(8,128)(2,1)S(1)}) custom-call(s32[3,27]{1,0:T(4,128)S(1)} %bitcast.16, s32[3,8]{1,0:T(4,128)S(1)} %bitcast.17, bf16[3,512,256]{2,1,0:T(8,128)(2,1)S(1)} %bitcast.14, bf16[3,64,256]{2,1,0:T(8,128)(2,1)S(1)} %collective-permute-done.low_ref, ...), custom_call_target="tpu_custom_call" | custom-call | flops 5435817984 | bytes 8388608 | tf_op jit(solution)/shard_map/input_gradient/pallas_call | solution.py:190
  30.6 3.4 %collective-permute-start.2 = (bf16[1,512,256]{2,1,0:T(8,128)(2,1)S(1)}, bf16[1,512,256]{2,1,0:T(8,128)(2,1)S(1)}, u32[]{:S(2)}, u32[]{:S(2)}) collective-permute-start(bf16[1,512,256]{2,1,0:T(8,128)(2,1)S(1)} %get-tuple-element.21), channel_id=1, source_target_pairs={{1,0},{2,1},{3,2},{4,3},{5,4},{6,5},{7,6},{0,7},{9,8},{10,9},{11,1... | collective-permute-start | bytes 786440 | tf_op jit(solution)/shard_map/ppermute | solution.py:479
  34.0 0.0 collective-permute-start.3
  34.0 5.2 %collective-permute-done.2.upper_ref = bf16[1,512,256]{2,1,0:T(8,128)(2,1)S(1)} collective-permute-done((bf16[1,512,256]{2,1,0:T(8,128)(2,1)S(1)}, bf16[1,512,256]{2,1,0:T(8,128)(2,1)S(1)}, u32[]{:S(2)}, u32[]{:S(2)}) %collective-permute-start.2) | collective-permute-done | bytes 262176 | tf_op jit(solution)/shard_map/ppermute | solution.py:479
  39.2 4.3 %collective-permute-done.3.lower_ref = bf16[1,512,256]{2,1,0:T(8,128)(2,1)S(1)} collective-permute-done((bf16[1,512,256]{2,1,0:T(8,128)(2,1)S(1)}, bf16[1,512,256]{2,1,0:T(8,128)(2,1)S(1)}, u32[]{:S(2)}, u32[]{:S(2)}) %collective-permute-start.3) | collective-permute-done | bytes 262176 | tf_op jit(solution)/shard_map/ppermute | solution.py:480
  43.5 0.0 copy-done.3
  43.5 0.0 copy-done.6
  43.5 4.1 %fine_gradient.1 = (bf16[24,512,128]{2,1,0:T(8,128)(2,1)}, bf16[4,256,128]{2,1,0:T(8,128)(2,1)S(1)}, bf16[4,256,128]{2,1,0:T(8,128)(2,1)S(1)}) custom-call(s32[2]{0:T(128)S(1)} %pad_add_fusion.where_ref, bf16[1,512,256]{2,1,0:T(8,128)(2,1)S(1)} %collective-permute-done.2.upper_ref, bf16[1,512,256]{2,1,0:T(8,128)(2,1)S(1)} %get-tuple-element.22.stay_ref, ...), custom_call_target="tpu_custom_call" | custom-call | flops 1610612736 | bytes 8388608 | tf_op jit(solution)/shard_map/fine_gradient/pallas_call | solution.py:336
  47.6 0.0 collective-permute-start.5
  47.6 1.5 %collective-permute-done.5.refs_3_ = bf16[4,256,128]{2,1,0:T(8,128)(2,1)S(1)} collective-permute-done((bf16[4,256,128]{2,1,0:T(8,128)(2,1)S(1)}, bf16[4,256,128]{2,1,0:T(8,128)(2,1)S(1)}, u32[]{:S(2)}, u32[]{:S(2)}) %collective-permute-start.5) | collective-permute-done | bytes 262176 | tf_op jit(solution)/shard_map/ppermute | solution.py:491
  49.1 0.0 collective-permute-done.4.refs_2_
  49.1 1.4 %pair_sum.1 = (f32[4,496,128]{2,1,0:T(8,128)S(1)}, bf16[4,496,128]{2,1,0:T(8,128)(2,1)S(1)}, bf16[4,496,128]{2,1,0:T(8,128)(2,1)S(1)}, bf16[4,496,128]{2,1,0:T(8,128)(2,1)S(1)}) custom-call(s32[2]{0:T(128)S(1)} %pad_add_fusion.where_ref, bf16[4,1728,128]{2,1,0:T(8,128)(2,1)S(1)} %get-tuple-element.25.refs_0_, ...), custom_call_target="tpu_custom_call" | custom-call | tf_op jit(solution)/shard_map/pair_sum/pallas_call | solution.py:374
  50.5 0.1 collective-permute-start.6
  50.6 0.5 collective-permute-start.7
  51.1 3.0 %collective-permute-start.8 = (bf16[4,496,128]{2,1,0:T(8,128)(2,1)S(1)}, bf16[4,496,128]{2,1,0:T(8,128)(2,1)S(1)}, u32[]{:S(2)}, u32[]{:S(2)}) collective-permute-start(bf16[4,496,128]{2,1,0:T(8,128)(2,1)S(1)} %get-tuple-element.32), channel_id=1, source_target_pairs={{0,6},{1,7},{2,4},{3,5},{4,2},{5,3},{6,0},{7,1},{8,14},{9,15},{10,... | collective-permute-start | bytes 1523720 | tf_op jit(solution)/shard_map/ppermute | solution.py:46
  54.1 10.9 %collective-permute-done.6.refs_1_ = bf16[4,496,128]{2,1,0:T(8,128)(2,1)S(1)} collective-permute-done((bf16[4,496,128]{2,1,0:T(8,128)(2,1)S(1)}, bf16[4,496,128]{2,1,0:T(8,128)(2,1)S(1)}, u32[]{:S(2)}, u32[]{:S(2)}) %collective-permute-start.6) | collective-permute-done | bytes 507936 | tf_op jit(solution)/shard_map/ppermute | solution.py:46
  65.0 10.2 %collective-permute-done.7.refs_2_ = bf16[4,496,128]{2,1,0:T(8,128)(2,1)S(1)} collective-permute-done((bf16[4,496,128]{2,1,0:T(8,128)(2,1)S(1)}, bf16[4,496,128]{2,1,0:T(8,128)(2,1)S(1)}, u32[]{:S(2)}, u32[]{:S(2)}) %collective-permute-start.7) | collective-permute-done | bytes 507936 | tf_op jit(solution)/shard_map/ppermute | solution.py:46
  75.2 0.0 collective-permute-done.8.refs_3_
  75.2 0.8 plane_sum.1
  76.0 1.6 %collective-permute-start.9 = (bf16[496,128]{1,0:T(8,128)(2,1)S(1)}, bf16[496,128]{1,0:T(8,128)(2,1)S(1)}, u32[]{:S(2)}, u32[]{:S(2)}) collective-permute-start(bf16[496,128]{1,0:T(8,128)(2,1)S(1)} %get-tuple-element.34), channel_id=1, source_target_pairs={{0,8},{8,0},{16,24},{24,16},{1,9},{9,1},{17,25},{25,17},{2,10},{10... | collective-permute-start | bytes 380936 | tf_op jit(solution)/shard_map/ppermute | solution.py:46
  77.6 2.6 %collective-permute-start.10 = (bf16[496,128]{1,0:T(8,128)(2,1)S(1)}, bf16[496,128]{1,0:T(8,128)(2,1)S(1)}, u32[]{:S(2)}, u32[]{:S(2)}) collective-permute-start(bf16[496,128]{1,0:T(8,128)(2,1)S(1)} %get-tuple-element.35), channel_id=1, source_target_pairs={{0,16},{8,24},{16,0},{24,8},{1,17},{9,25},{17,1},{25,9},{2,18},{10... | collective-permute-start | bytes 380936 | tf_op jit(solution)/shard_map/ppermute | solution.py:46
  80.2 0.2 collective-permute-start.11
  80.4 1.9 %collective-permute-done.9.refs_1_ = bf16[496,128]{1,0:T(8,128)(2,1)S(1)} collective-permute-done((bf16[496,128]{1,0:T(8,128)(2,1)S(1)}, bf16[496,128]{1,0:T(8,128)(2,1)S(1)}, u32[]{:S(2)}, u32[]{:S(2)}) %collective-permute-start.9) | collective-permute-done | bytes 127008 | tf_op jit(solution)/shard_map/ppermute | solution.py:46
  82.4 7.2 %collective-permute-done.10.refs_2_ = bf16[496,128]{1,0:T(8,128)(2,1)S(1)} collective-permute-done((bf16[496,128]{1,0:T(8,128)(2,1)S(1)}, bf16[496,128]{1,0:T(8,128)(2,1)S(1)}, u32[]{:S(2)}, u32[]{:S(2)}) %collective-permute-start.10) | collective-permute-done | bytes 127008 | tf_op jit(solution)/shard_map/ppermute | solution.py:46
  89.6 0.0 collective-permute-done.11.refs_3_
  89.6 0.1 slab_sum.1.refs_0_
  89.7 1.7 %collective-permute-start.14 = (bf16[496,128]{1,0:T(8,128)(2,1)S(1)}, bf16[496,128]{1,0:T(8,128)(2,1)S(1)}, u32[]{:S(2)}, u32[]{:S(2)}) collective-permute-start(bf16[496,128]{1,0:T(8,128)(2,1)S(1)} %slab_sum.1.refs_0_), channel_id=1, source_target_pairs={{0,6},{1,7},{2,4},{3,5},{4,2},{5,3},{6,0},{7,1},{8,14},{9,15},{10,... | collective-permute-start | bytes 380936 | tf_op jit(solution)/shard_map/ppermute | solution.py:46
  91.3 1.3 %collective-permute-start.13 = (bf16[496,128]{1,0:T(8,128)(2,1)S(1)}, bf16[496,128]{1,0:T(8,128)(2,1)S(1)}, u32[]{:S(2)}, u32[]{:S(2)}) collective-permute-start(bf16[496,128]{1,0:T(8,128)(2,1)S(1)} %slab_sum.1.refs_0_), channel_id=1, source_target_pairs={{0,4},{1,5},{2,6},{3,7},{4,0},{5,1},{6,2},{7,3},{8,12},{9,13},{10,... | collective-permute-start | bytes 380936 | tf_op jit(solution)/shard_map/ppermute | solution.py:46
  92.7 0.6 collective-permute-start.12
  93.2 0.0 collective-permute-start.15
  93.2 2.4 %collective-permute-done.14.refs_3_ = bf16[496,128]{1,0:T(8,128)(2,1)S(1)} collective-permute-done((bf16[496,128]{1,0:T(8,128)(2,1)S(1)}, bf16[496,128]{1,0:T(8,128)(2,1)S(1)}, u32[]{:S(2)}, u32[]{:S(2)}) %collective-permute-start.14) | collective-permute-done | bytes 127008 | tf_op jit(solution)/shard_map/ppermute | solution.py:46
  95.6 0.0 collective-permute-start.18
  95.6 1.3 %collective-permute-done.13.refs_2_ = bf16[496,128]{1,0:T(8,128)(2,1)S(1)} collective-permute-done((bf16[496,128]{1,0:T(8,128)(2,1)S(1)}, bf16[496,128]{1,0:T(8,128)(2,1)S(1)}, u32[]{:S(2)}, u32[]{:S(2)}) %collective-permute-start.13) | collective-permute-done | bytes 127008 | tf_op jit(solution)/shard_map/ppermute | solution.py:46
  96.9 0.0 collective-permute-start.17
  96.9 0.7 collective-permute-done.12.refs_1_
  97.6 0.0 collective-permute-start.16
  97.6 0.0 collective-permute-done.15.refs_4_
  97.6 0.0 collective-permute-done.18.refs_7_
  97.6 0.7 collective-permute-done.17.refs_6_
  98.3 0.7 collective-permute-done.16.refs_5_
  98.9 2.1 %gather_up.1 = (f32[1728,256]{1,0:T(8,128)}, f32[256,256]{1,0:T(8,128)}) custom-call(s32[2]{0:T(128)S(1)} %pad_add_fusion.where_ref, bf16[496,128]{1,0:T(8,128)(2,1)S(1)} %slab_sum.1.refs_0_, bf16[496,128]{1,0:T(8,128)(2,1)S(1)} %collective-permute-done.12.refs_1_, bf16[496,128]{1,0:T(8,128)(2,1)S(1)} %collective-permute-done.13.refs_2_, ...), custom_call_target="tpu_custom_call" | custom-call | tf_op jit(solution)/shard_map/gather_up/pallas_call | solution.py:448
  (1 shorter events, 0.0 us)
Async XLA Ops:
  1.6 5.1 %collective-permute-start.1 = (bf16[3,64,256]{2,1,0:T(8,128)(2,1)S(1)}, bf16[3,64,256]{2,1,0:T(8,128)(2,1)S(1)}, u32[]{:S(2)}, u32[]{:S(2)}) collective-permute-start(bf16[3,64,256]{2,1,0:T(8,128)(2,1)S(1)} %get-tuple-element.39), channel_id=1, source_target_pairs={{1,0},{2,1},{3,2},{4,3},{5,4},{6,5},{7,6},{9,8},{10,9},{11,10},{12... | collective-permute-start | bytes 294920 | tf_op jit(solution)/shard_map/ppermute | solution.py:475
  2.9 4.0 %collective-permute-start = (bf16[3,64,256]{2,1,0:T(8,128)(2,1)S(1)}, bf16[3,64,256]{2,1,0:T(8,128)(2,1)S(1)}, u32[]{:S(2)}, u32[]{:S(2)}) collective-permute-start(bf16[3,64,256]{2,1,0:T(8,128)(2,1)S(1)} %get-tuple-element.40), channel_id=1, source_target_pairs={{0,1},{1,2},{2,3},{3,4},{4,5},{5,6},{6,7},{8,9},{9,10},{10,11},{11... | collective-permute-start | bytes 294920 | tf_op jit(solution)/shard_map/ppermute | solution.py:474
  6.9 1.1 %copy-start = (bf16[1,3,512,256]{3,2,1,0:T(8,128)(2,1)S(1)}, bf16[1,3,512,256]{3,2,1,0:T(8,128)(2,1)}, u32[]{:S(2)}) copy-start(bf16[1,3,512,256]{3,2,1,0:T(8,128)(2,1)} %param.7) | copy-start | bytes 2359300
  8.0 1.1 %copy-start.4 = (bf16[1,3,512,256]{3,2,1,0:T(8,128)(2,1)S(1)}, bf16[1,3,512,256]{3,2,1,0:T(8,128)(2,1)}, u32[]{:S(2)}) copy-start(bf16[1,3,512,256]{3,2,1,0:T(8,128)(2,1)} %param.8) | copy-start | bytes 2359300
  9.1 12.0 %copy-start.7 = (s32[1,1,3,8]{3,1,2,0:T(1,128)S(1)}, s32[1,1,3,8]{3,1,2,0:T(1,128)}, u32[]{:S(2)}) copy-start(s32[1,1,3,8]{3,1,2,0:T(1,128)} %param.13) | copy-start | bytes 292
  9.1 12.0 %copy-start.1 = (bf16[1,3,512,256]{3,2,1,0:T(8,128)(2,1)S(1)}, bf16[1,3,512,256]{3,2,1,0:T(8,128)(2,1)}, u32[]{:S(2)}) copy-start(bf16[1,3,512,256]{3,2,1,0:T(8,128)(2,1)} %param.7) | copy-start | bytes 2359300
  9.1 12.0 %copy-start.2 = (bf16[27,256,256]{2,1,0:T(8,128)(2,1)S(1)}, bf16[27,256,256]{2,1,0:T(8,128)(2,1)}, u32[]{:S(2)}) copy-start(bf16[27,256,256]{2,1,0:T(8,128)(2,1)} %weight_ref.2) | copy-start | bytes 10616836
  9.1 12.0 %copy-start.5 = (bf16[1,3,512,256]{3,2,1,0:T(8,128)(2,1)S(1)}, bf16[1,3,512,256]{3,2,1,0:T(8,128)(2,1)}, u32[]{:S(2)}) copy-start(bf16[1,3,512,256]{3,2,1,0:T(8,128)(2,1)} %param.8) | copy-start | bytes 2359300
  17.8 31.3 %collective-permute-start.4 = (bf16[4,1728,128]{2,1,0:T(8,128)(2,1)S(1)}, bf16[4,1728,128]{2,1,0:T(8,128)(2,1)S(1)}, u32[]{:S(2)}, u32[]{:S(2)}) collective-permute-start(bf16[4,1728,128]{2,1,0:T(8,128)(2,1)S(1)} %get-tuple-element.27), channel_id=1, source_target_pairs={{0,1},{1,0},{2,3},{3,2},{4,5},{5,4},{6,7},{7,6},{8,9},{9,8},{10,11... | collective-permute-start | bytes 5308424 | tf_op jit(solution)/shard_map/ppermute | solution.py:490
  21.1 22.4 %copy-start.3 = (bf16[1,24,512,128]{3,2,1,0:T(8,128)(2,1)S(1)}, bf16[1,24,512,128]{3,2,1,0:T(8,128)(2,1)}, u32[]{:S(2)}) copy-start(bf16[1,24,512,128]{3,2,1,0:T(8,128)(2,1)} %param.11) | copy-start | bytes 9437188
  21.1 22.3 %copy-start.6 = (bf16[8,128,256]{2,1,0:T(8,128)(2,1)S(1)}, bf16[8,128,256]{2,1,0:T(8,128)(2,1)}, u32[]{:S(2)}) copy-start(bf16[8,128,256]{2,1,0:T(8,128)(2,1)} %weight_ref.3) | copy-start | bytes 1572868
  30.6 8.6 %collective-permute-start.2 = (bf16[1,512,256]{2,1,0:T(8,128)(2,1)S(1)}, bf16[1,512,256]{2,1,0:T(8,128)(2,1)S(1)}, u32[]{:S(2)}, u32[]{:S(2)}) collective-permute-start(bf16[1,512,256]{2,1,0:T(8,128)(2,1)S(1)} %get-tuple-element.21), channel_id=1, source_target_pairs={{1,0},{2,1},{3,2},{4,3},{5,4},{6,5},{7,6},{0,7},{9,8},{10,9},{11,1... | collective-permute-start | bytes 786440 | tf_op jit(solution)/shard_map/ppermute | solution.py:479
  34.0 9.5 %collective-permute-start.3 = (bf16[1,512,256]{2,1,0:T(8,128)(2,1)S(1)}, bf16[1,512,256]{2,1,0:T(8,128)(2,1)S(1)}, u32[]{:S(2)}, u32[]{:S(2)}) collective-permute-start(bf16[1,512,256]{2,1,0:T(8,128)(2,1)S(1)} %get-tuple-element.23), channel_id=1, source_target_pairs={{0,1},{1,2},{2,3},{3,4},{4,5},{5,6},{6,7},{7,0},{8,9},{9,10},{10,1... | collective-permute-start | bytes 786440 | tf_op jit(solution)/shard_map/ppermute | solution.py:480
  47.6 1.5 %collective-permute-start.5 = (bf16[4,256,128]{2,1,0:T(8,128)(2,1)S(1)}, bf16[4,256,128]{2,1,0:T(8,128)(2,1)S(1)}, u32[]{:S(2)}, u32[]{:S(2)}) collective-permute-start(bf16[4,256,128]{2,1,0:T(8,128)(2,1)S(1)} %get-tuple-element.28), channel_id=1, source_target_pairs={{0,1},{1,0},{2,3},{3,2},{4,5},{5,4},{6,7},{7,6},{8,9},{9,8},{10,11... | collective-permute-start | bytes 786440 | tf_op jit(solution)/shard_map/ppermute | solution.py:491
  50.5 14.5 %collective-permute-start.6 = (bf16[4,496,128]{2,1,0:T(8,128)(2,1)S(1)}, bf16[4,496,128]{2,1,0:T(8,128)(2,1)S(1)}, u32[]{:S(2)}, u32[]{:S(2)}) collective-permute-start(bf16[4,496,128]{2,1,0:T(8,128)(2,1)S(1)} %get-tuple-element.30), channel_id=1, source_target_pairs={{0,2},{1,3},{2,0},{3,1},{4,6},{5,7},{6,4},{7,5},{8,10},{9,11},{10,... | collective-permute-start | bytes 1523720 | tf_op jit(solution)/shard_map/ppermute | solution.py:46
  50.6 24.6 %collective-permute-start.7 = (bf16[4,496,128]{2,1,0:T(8,128)(2,1)S(1)}, bf16[4,496,128]{2,1,0:T(8,128)(2,1)S(1)}, u32[]{:S(2)}, u32[]{:S(2)}) collective-permute-start(bf16[4,496,128]{2,1,0:T(8,128)(2,1)S(1)} %get-tuple-element.31), channel_id=1, source_target_pairs={{0,4},{1,5},{2,6},{3,7},{4,0},{5,1},{6,2},{7,3},{8,12},{9,13},{10,... | collective-permute-start | bytes 1523720 | tf_op jit(solution)/shard_map/ppermute | solution.py:46
  51.1 24.1 %collective-permute-start.8 = (bf16[4,496,128]{2,1,0:T(8,128)(2,1)S(1)}, bf16[4,496,128]{2,1,0:T(8,128)(2,1)S(1)}, u32[]{:S(2)}, u32[]{:S(2)}) collective-permute-start(bf16[4,496,128]{2,1,0:T(8,128)(2,1)S(1)} %get-tuple-element.32), channel_id=1, source_target_pairs={{0,6},{1,7},{2,4},{3,5},{4,2},{5,3},{6,0},{7,1},{8,14},{9,15},{10,... | collective-permute-start | bytes 1523720 | tf_op jit(solution)/shard_map/ppermute | solution.py:46
  76.0 6.4 %collective-permute-start.9 = (bf16[496,128]{1,0:T(8,128)(2,1)S(1)}, bf16[496,128]{1,0:T(8,128)(2,1)S(1)}, u32[]{:S(2)}, u32[]{:S(2)}) collective-permute-start(bf16[496,128]{1,0:T(8,128)(2,1)S(1)} %get-tuple-element.34), channel_id=1, source_target_pairs={{0,8},{8,0},{16,24},{24,16},{1,9},{9,1},{17,25},{25,17},{2,10},{10... | collective-permute-start | bytes 380936 | tf_op jit(solution)/shard_map/ppermute | solution.py:46
  77.6 12.0 %collective-permute-start.10 = (bf16[496,128]{1,0:T(8,128)(2,1)S(1)}, bf16[496,128]{1,0:T(8,128)(2,1)S(1)}, u32[]{:S(2)}, u32[]{:S(2)}) collective-permute-start(bf16[496,128]{1,0:T(8,128)(2,1)S(1)} %get-tuple-element.35), channel_id=1, source_target_pairs={{0,16},{8,24},{16,0},{24,8},{1,17},{9,25},{17,1},{25,9},{2,18},{10... | collective-permute-start | bytes 380936 | tf_op jit(solution)/shard_map/ppermute | solution.py:46
  80.2 9.4 %collective-permute-start.11 = (bf16[496,128]{1,0:T(8,128)(2,1)S(1)}, bf16[496,128]{1,0:T(8,128)(2,1)S(1)}, u32[]{:S(2)}, u32[]{:S(2)}) collective-permute-start(bf16[496,128]{1,0:T(8,128)(2,1)S(1)} %get-tuple-element.36), channel_id=1, source_target_pairs={{0,24},{8,16},{16,8},{24,0},{1,25},{9,17},{17,9},{25,1},{2,26},{10... | collective-permute-start | bytes 380936 | tf_op jit(solution)/shard_map/ppermute | solution.py:46
  89.7 6.0 %collective-permute-start.14 = (bf16[496,128]{1,0:T(8,128)(2,1)S(1)}, bf16[496,128]{1,0:T(8,128)(2,1)S(1)}, u32[]{:S(2)}, u32[]{:S(2)}) collective-permute-start(bf16[496,128]{1,0:T(8,128)(2,1)S(1)} %slab_sum.1.refs_0_), channel_id=1, source_target_pairs={{0,6},{1,7},{2,4},{3,5},{4,2},{5,3},{6,0},{7,1},{8,14},{9,15},{10,... | collective-permute-start | bytes 380936 | tf_op jit(solution)/shard_map/ppermute | solution.py:46
  91.3 5.6 %collective-permute-start.13 = (bf16[496,128]{1,0:T(8,128)(2,1)S(1)}, bf16[496,128]{1,0:T(8,128)(2,1)S(1)}, u32[]{:S(2)}, u32[]{:S(2)}) collective-permute-start(bf16[496,128]{1,0:T(8,128)(2,1)S(1)} %slab_sum.1.refs_0_), channel_id=1, source_target_pairs={{0,4},{1,5},{2,6},{3,7},{4,0},{5,1},{6,2},{7,3},{8,12},{9,13},{10,... | collective-permute-start | bytes 380936 | tf_op jit(solution)/shard_map/ppermute | solution.py:46
  92.7 4.9 %collective-permute-start.12 = (bf16[496,128]{1,0:T(8,128)(2,1)S(1)}, bf16[496,128]{1,0:T(8,128)(2,1)S(1)}, u32[]{:S(2)}, u32[]{:S(2)}) collective-permute-start(bf16[496,128]{1,0:T(8,128)(2,1)S(1)} %slab_sum.1.refs_0_), channel_id=1, source_target_pairs={{0,2},{1,3},{2,0},{3,1},{4,6},{5,7},{6,4},{7,5},{8,10},{9,11},{10,... | collective-permute-start | bytes 380936 | tf_op jit(solution)/shard_map/ppermute | solution.py:46
  93.2 4.4 %collective-permute-start.15 = (bf16[496,128]{1,0:T(8,128)(2,1)S(1)}, bf16[496,128]{1,0:T(8,128)(2,1)S(1)}, u32[]{:S(2)}, u32[]{:S(2)}) collective-permute-start(bf16[496,128]{1,0:T(8,128)(2,1)S(1)} %slab_sum.1.refs_0_), channel_id=1, source_target_pairs={{0,1},{1,0},{2,3},{3,2},{4,5},{5,4},{6,7},{7,6},{8,9},{9,8},{10,11... | collective-permute-start | bytes 380936 | tf_op jit(solution)/shard_map/ppermute | solution.py:499
  95.6 2.0 %collective-permute-start.18 = (bf16[496,128]{1,0:T(8,128)(2,1)S(1)}, bf16[496,128]{1,0:T(8,128)(2,1)S(1)}, u32[]{:S(2)}, u32[]{:S(2)}) collective-permute-start(bf16[496,128]{1,0:T(8,128)(2,1)S(1)} %collective-permute-done.14.refs_3_), channel_id=1, source_target_pairs={{0,1},{1,0},{2,3},{3,2},{4,5},{5,4},{6,7},{7,6},{8,9},{9,8},{10,11... | collective-permute-start | bytes 380936 | tf_op jit(solution)/shard_map/ppermute | solution.py:499
  96.9 1.3 %collective-permute-start.17 = (bf16[496,128]{1,0:T(8,128)(2,1)S(1)}, bf16[496,128]{1,0:T(8,128)(2,1)S(1)}, u32[]{:S(2)}, u32[]{:S(2)}) collective-permute-start(bf16[496,128]{1,0:T(8,128)(2,1)S(1)} %collective-permute-done.13.refs_2_), channel_id=1, source_target_pairs={{0,1},{1,0},{2,3},{3,2},{4,5},{5,4},{6,7},{7,6},{8,9},{9,8},{10,11... | collective-permute-start | bytes 380936 | tf_op jit(solution)/shard_map/ppermute | solution.py:499
  97.6 1.3 %collective-permute-start.16 = (bf16[496,128]{1,0:T(8,128)(2,1)S(1)}, bf16[496,128]{1,0:T(8,128)(2,1)S(1)}, u32[]{:S(2)}, u32[]{:S(2)}) collective-permute-start(bf16[496,128]{1,0:T(8,128)(2,1)S(1)} %collective-permute-done.12.refs_1_), channel_id=1, source_target_pairs={{0,1},{1,0},{2,3},{3,2},{4,5},{5,4},{6,7},{7,6},{8,9},{9,8},{10,11... | collective-permute-start | bytes 380936 | tf_op jit(solution)/shard_map/ppermute | solution.py:499

commit v2 on v1

--- a/solution.py
+++ b/solution.py
@@ -104,7 +104,7 @@
 
 
 def input_kernel(
-    links_ref, routes_ref, own_ref, low_ref, high_ref, pre_ref, weight_ref,
+    links_ref, routes_ref, own_ref, low_ref, high_ref, pre_ref, weight_ref, after_ref,
     to_lower_ref, stay_ref, to_upper_ref,
     win_ref, taps_ref, acc_ref, octants_ref, tap_sems, out_sems,
 ):
@@ -182,7 +182,7 @@
         copy.wait()
 
 
-def input_gradient(links, routes, own, low, high, pre, weight):
+def input_gradient(links, routes, own, low, high, pre, weight, after):
     slots, voxels, channels = own.shape
     groups = routes.shape[1] // 8
     rows = slots * voxels
@@ -190,7 +190,7 @@
     return pl.pallas_call(
         input_kernel,
         out_shape=(out, out, out),
-        in_specs=[SMEM, SMEM, VMEM, VMEM, VMEM, VMEM, ANY],
+        in_specs=[SMEM, SMEM, VMEM, VMEM, VMEM, VMEM, ANY, ANY],
         out_specs=(ANY, ANY, ANY),
         scratch_shapes=[
             pltpu.VMEM((slots * PLANE * (BE + 2), 9 * channels), BF16),
@@ -205,12 +205,12 @@
             flops=2 * rows * 27 * channels * channels, bytes_accessed=8 * MIB, transcendentals=0
         ),
         name="input_gradient",
-    )(links, routes, own, low, high, pre, weight)
+    )(links, routes, own, low, high, pre, weight, after)
 
 
 def filter_kernel(
-    shard_rows, where_ref, links_ref, own_ref, low_ref, high_ref, pre_ref,
-    keep_ref, send_ref, win_ref, act_ref,
+    shard_rows, links_ref, own_ref, low_ref, high_ref, pre_ref,
+    keep_a_ref, keep_b_ref, send_a_ref, send_b_ref, win_ref, act_ref,
 ):
     slots, voxels, channels = own_ref.shape
     slab = slots * PLANE
@@ -224,8 +224,9 @@
         block = jnp.maximum(jnp.concatenate(parts, axis=0).astype(F32), 0.0)
         act_ref[:, pair * 2 * slab : (pair + 1) * 2 * slab] = block.T.astype(BF16)
     build_windows(links_ref, own_ref, low_ref, high_ref, win_ref)
-    first = lax.rem(where_ref[0], 2) == 0
+    first = lax.rem(lax.axis_index("dom"), 2) == 0
     unit = math.gcd(channels, shard_rows)
+    cut = keep_a_ref.shape[1]
 
     def step(index_x, carry):
         offset = pl.multiple_of((2 - index_x) * slab, PLANE)
@@ -243,23 +244,39 @@
                 shard = row // shard_rows
                 start = pl.multiple_of(row - shard * shard_rows, unit)
                 span = slice(part * unit, (part + 1) * unit)
-                keep_ref[shard, pl.ds(start, unit), :] = keep[span]
-                send_ref[shard, pl.ds(start, unit), :] = send[span]
+                @pl.when(start < cut)
+                def _():
+                    keep_a_ref[shard, pl.ds(start, unit), :] = keep[span]
+                    send_a_ref[shard, pl.ds(start, unit), :] = send[span]
+
+                @pl.when(start >= cut)
+                def _():
+                    late = pl.multiple_of(start - cut, unit)
+                    keep_b_ref[shard, pl.ds(late, unit), :] = keep[span]
+                    send_b_ref[shard, pl.ds(late, unit), :] = send[span]
+
         return carry
 
     lax.fori_loop(0, 3, step, 0)
 
 
-def filter_gradient(shards, where, links, own, low, high, pre):
+def piece_rows(rows, count):
+    return -(-rows // (16 * count)) * 16
+
+
+def filter_gradient(shards, count, links, own, low, high, pre):
     slots, voxels, channels = own.shape
     shard_rows = 27 * channels // shards
     rows = slots * voxels
-    out = jax.ShapeDtypeStruct((shards, shard_rows, channels // 2), BF16)
+    cut = count * piece_rows(shard_rows // 2, count)
+    rest = count * piece_rows(shard_rows - cut, count)
+    first = jax.ShapeDtypeStruct((shards, cut, channels // 2), BF16)
+    second = jax.ShapeDtypeStruct((shards, rest, channels // 2), BF16)
     return pl.pallas_call(
         functools.partial(filter_kernel, shard_rows),
-        out_shape=(out, out),
-        in_specs=[SMEM, SMEM, VMEM, VMEM, VMEM, VMEM],
-        out_specs=(VMEM, VMEM),
+        out_shape=(first, second, first, second),
+        in_specs=[SMEM, VMEM, VMEM, VMEM, VMEM],
+        out_specs=(VMEM, VMEM, VMEM, VMEM),
         scratch_shapes=[
             pltpu.VMEM((slots * PLANE * (BE + 2), 9 * channels), BF16),
             pltpu.VMEM((channels, rows), BF16),
@@ -269,11 +286,11 @@
             flops=2 * rows * 27 * channels * channels, bytes_accessed=8 * MIB, transcendentals=0
         ),
         name="filter_gradient",
-    )(where, links, own, low, high, pre)
+    )(links, own, low, high, pre)
 
 
 def fine_kernel(
-    where_ref, upper_ref, stay_ref, lower_ref, weight_ref, act_ref,
+    upper_ref, stay_ref, lower_ref, weight_ref, act_ref,
     grad_ref, keep_ref, send_ref, acc_ref,
 ):
     step = pl.program_id(0)
@@ -316,21 +333,29 @@
 
     @pl.when(step == pl.num_programs(0) - 1)
     def _():
-        first = lax.rem(where_ref[0], 2) == 0
+        first = lax.rem(lax.axis_index("dom"), 2) == 0
         total = acc_ref[...].T
         lanes = channels // 2
         left, right = total[:, :lanes], total[:, lanes:]
-        keep_ref[...] = jnp.where(first, left, right).astype(BF16).reshape(keep_ref.shape)
-        send_ref[...] = jnp.where(first, right, left).astype(BF16).reshape(send_ref.shape)
-
-
-def fine_gradient(shards, where, from_upper, stay, from_lower, weight, fine_act):
+        shards = keep_ref.shape[0]
+        rows = total.shape[0] // shards
+        keep_ref[:, :rows, :] = (
+            jnp.where(first, left, right).astype(BF16).reshape(shards, rows, lanes)
+        )
+        send_ref[:, :rows, :] = (
+            jnp.where(first, right, left).astype(BF16).reshape(shards, rows, lanes)
+        )
+
+
+def fine_gradient(shards, count, from_upper, stay, from_lower, weight, fine_act):
     fine, voxels, fine_channels = fine_act.shape
     groups, _, channels = stay.shape
     taps = weight.shape[0]
     per_row = 8
     whole = pl.BlockSpec((1, voxels, channels), lambda i: (0, 0, 0))
-    out = jax.ShapeDtypeStruct((shards, taps * fine_channels // shards, channels // 2), BF16)
+    rows = taps * fine_channels // shards
+    padded = count * piece_rows(rows, count)
+    out = jax.ShapeDtypeStruct((shards, padded, channels // 2), BF16)
     same = pl.BlockSpec(out.shape, lambda i: (0, 0, 0))
     block = pl.BlockSpec((per_row, voxels, fine_channels), lambda i: (i, 0, 0))
     return pl.pallas_call(
@@ -338,7 +363,7 @@
         grid=(3,),
         out_shape=(jax.ShapeDtypeStruct(fine_act.shape, BF16), out, out),
         in_specs=[
-            SMEM, whole, whole, whole,
+            whole, whole, whole,
             pl.BlockSpec(weight.shape, lambda i: (0, 0, 0)),
             block,
         ],
@@ -350,62 +375,70 @@
             transcendentals=0,
         ),
         name="fine_gradient",
-    )(where, from_upper, stay, from_lower, weight, fine_act)
-
-
-def pair_kernel(count, piece, where_ref, *refs):
-    keeps, gots, outs = refs[:2], refs[2:4], refs[4 : 4 + count]
-    scratch = refs[4 + count]
-    shards = scratch.shape[0]
-    start = 0
-    for keep_ref, got_ref in zip(keeps, gots):
-        rows = keep_ref.shape[1]
-        scratch[:, start : start + rows, :] = keep_ref[...].astype(F32) + got_ref[...].astype(F32)
-        start += rows
-    high = where_ref[0] // 2
+    )(from_upper, stay, from_lower, weight, fine_act)
+
+
+def cost(*arrays):
+    moved = sum(math.prod(x.shape) * jnp.dtype(x.dtype).itemsize for x in arrays)
+    return pl.CostEstimate(flops=moved, bytes_accessed=moved, transcendentals=0)
+
+
+def pair_kernel(count, keep_ref, got_ref, *outs):
+    piece = outs[0].shape[1]
+    high = lax.axis_index("dom") // 2
     for step, ref in enumerate(outs):
-        row = pl.multiple_of(relative(high, step, count) * piece, 16)
-        ref[...] = scratch[:, pl.ds(row, piece), :].astype(ref.dtype)
-
-
-def pair_sum(where, count, piece, keeps, gots):
-    shards, _, lanes = keeps[0].shape
-    shape = (shards, piece, lanes)
-    return pl.pallas_call(
-        functools.partial(pair_kernel, count, piece),
-        out_shape=[jax.ShapeDtypeStruct(shape, F32 if step == 0 else BF16) for step in range(count)],
-        in_specs=[SMEM] + [VMEM] * 4,
+        rows = pl.ds(pl.multiple_of(relative(high, step, count) * piece, 16), piece)
+        total = keep_ref[:, rows, :].astype(F32) + got_ref[:, rows, :].astype(F32)
+        ref[...] = total.astype(ref.dtype)
+
+
+def pair_sum(count, keep, got):
+    shards, rows, lanes = keep.shape
+    shape = (shards, rows // count, lanes)
+    outs = [jax.ShapeDtypeStruct(shape, F32 if step == 0 else BF16) for step in range(count)]
+    return pl.pallas_call(
+        functools.partial(pair_kernel, count),
+        out_shape=outs,
+        in_specs=[VMEM] * 2,
         out_specs=[VMEM] * count,
-        scratch_shapes=[pltpu.VMEM((shards, piece * count, lanes), F32)],
-        compiler_params=params(40),
+        compiler_params=params(32),
+        cost_estimate=cost(keep, got, *outs),
         name="pair_sum",
-    )(where, *keeps, *gots)
-
-
-def plane_kernel(count, where_ref, *refs):
-    shards = refs[0].shape[0]
-    outs = refs[count:]
+    )(keep, got)
+
+
+def plane_kernel(count, streams, *refs):
+    parts, outs = refs[: count * streams], refs[count * streams :]
+    shards = parts[0].shape[0]
     for step, ref in enumerate(outs):
-        shard = relative(where_ref[1], step, shards)
-        total = refs[0][shard].astype(F32)
-        for part in refs[1:count]:
-            total = total + part[shard].astype(F32)
-        ref[...] = total.astype(ref.dtype)
-
-
-def plane_sum(where, parts):
-    shards, piece, lanes = parts[0].shape
-    return pl.pallas_call(
-        functools.partial(plane_kernel, len(parts)),
-        out_shape=[
-            jax.ShapeDtypeStruct((piece, lanes), F32 if step == 0 else BF16)
-            for step in range(shards)
-        ],
-        in_specs=[SMEM] + [VMEM] * len(parts),
+        shard = relative(lax.axis_index("dp"), step, shards)
+        start = 0
+        for stream in range(streams):
+            group = parts[stream * count : (stream + 1) * count]
+            total = group[0][shard].astype(F32)
+            for part in group[1:]:
+                total = total + part[shard].astype(F32)
+            rows = total.shape[0]
+            ref[start : start + rows, :] = total.astype(ref.dtype)
+            start += rows
+
+
+def plane_sum(streams):
+    parts = [part for stream in streams for part in stream]
+    shards, _, lanes = parts[0].shape
+    piece = sum(stream[0].shape[1] for stream in streams)
+    outs = [
+        jax.ShapeDtypeStruct((piece, lanes), F32 if step == 0 else BF16) for step in range(shards)
+    ]
+    return pl.pallas_call(
+        functools.partial(plane_kernel, len(streams[0]), len(streams)),
+        out_shape=outs,
+        in_specs=[VMEM] * len(parts),
         out_specs=[VMEM] * shards,
-        compiler_params=params(40),
+        compiler_params=params(32),
+        cost_estimate=cost(*parts, *outs),
         name="plane_sum",
-    )(where, *parts)
+    )(*parts)
 
 
 def slab_kernel(factor, *refs):
@@ -421,42 +454,54 @@
         out_shape=jax.ShapeDtypeStruct(parts[0].shape, BF16),
         in_specs=[VMEM] * len(parts),
         out_specs=VMEM,
-        compiler_params=params(40),
+        compiler_params=params(32),
+        cost_estimate=cost(*parts),
         name="slab_sum",
     )(*parts)
 
 
-def gather_kernel(count, where_ref, *refs):
-    near, far = refs[:count], refs[count : 2 * count]
-    conv_ref, down_ref, scratch = refs[2 * count :]
-    piece, lanes = near[0].shape
-    high = where_ref[0] // 2
-    low = lax.rem(where_ref[0], 2)
-    for side, parts in ((low, near), (1 - low, far)):
-        lane = pl.multiple_of(side * lanes, lanes)
-        for step, ref in enumerate(parts):
-            row = pl.multiple_of(source_of(high, step, count) * piece, 16)
-            scratch[pl.ds(row, piece), pl.ds(lane, lanes)] = ref[...].astype(F32)
-    conv_rows = conv_ref.shape[0]
-    conv_ref[...] = scratch[:conv_rows]
-    down_ref[...] = scratch[conv_rows : conv_rows + down_ref.shape[0]]
-
-
-def gather_up(where, conv_rows, down_rows, near, far):
-    piece, lanes = near[0].shape
-    count = len(near)
-    return pl.pallas_call(
-        functools.partial(gather_kernel, count),
-        out_shape=(
-            jax.ShapeDtypeStruct((conv_rows, 2 * lanes), F32),
-            jax.ShapeDtypeStruct((down_rows, 2 * lanes), F32),
-        ),
-        in_specs=[SMEM] + [VMEM] * (2 * count),
-        out_specs=(VMEM, VMEM),
-        scratch_shapes=[pltpu.VMEM((count * piece, 2 * lanes), F32)],
-        compiler_params=params(40),
+def gather_kernel(count, layout, *refs):
+    inputs = refs[: 2 * count * len(layout)]
+    conv_ref, down_ref, *scratches = refs[len(inputs) :]
+    lanes = inputs[0].shape[1]
+    high = lax.axis_index("dom") // 2
+    low = lax.rem(lax.axis_index("dom"), 2)
+    scratch = iter(scratches)
+    for chunk, streams in enumerate(layout):
+        parts = inputs[2 * count * chunk : 2 * count * (chunk + 1)]
+        start = 0
+        for output, first, piece in streams:
+            whole = next(scratch)
+            for side, group in ((low, parts[:count]), (1 - low, parts[count:])):
+                lane = pl.ds(pl.multiple_of(side * lanes, lanes), lanes)
+                for step, ref in enumerate(group):
+                    row = pl.multiple_of(source_of(high, step, count) * piece, 16)
+                    whole[pl.ds(row, piece), lane] = ref[start : start + piece, :].astype(F32)
+            out_ref = (conv_ref, down_ref)[output]
+            rows = min(count * piece, out_ref.shape[0] - first)
+            out_ref[first : first + rows, :] = whole[:rows, :]
+            start += piece
+
+
+def gather_up(shapes, layout, chunks):
+    inputs = [part for near, far in chunks for part in near + far]
+    count = len(chunks[0][0])
+    lanes = inputs[0].shape[1]
+    outs = [jax.ShapeDtypeStruct(shape, F32) for shape in shapes]
+    return pl.pallas_call(
+        functools.partial(gather_kernel, count, layout),
+        out_shape=outs,
+        in_specs=[VMEM] * len(inputs),
+        out_specs=[VMEM] * 2,
+        scratch_shapes=[
+            pltpu.VMEM((count * piece, 2 * lanes), F32)
+            for streams in layout
+            for _, _, piece in streams
+        ],
+        compiler_params=params(32),
+        cost_estimate=cost(*inputs, *outs),
         name="gather_up",
-    )(where, *near, *far)
+    )(*inputs)
 
 
 def body(grad_out, pre_act, conv_weight, down_weight, fine_act, neighbours, octant_routes):
@@ -467,37 +512,49 @@
     slots, voxels, channels = own.shape
     devices = lax.axis_size("dom")
     shards = lax.axis_size("dp")
-    where = jnp.stack([lax.axis_index("dom"), lax.axis_index("dp")]).astype(jnp.int32)
 
     forward = [(i, i + 1) for i in range(devices - 1)]
     backward = [(i + 1, i) for i in range(devices - 1)]
     low = lax.ppermute(own[:, voxels - PLANE :], "dom", forward)
     high = lax.ppermute(own[:, :PLANE], "dom", backward)
 
-    to_lower, stay, to_upper = input_gradient(links, routes, own, low, high, pre, conv_weight)
+    count = devices // 2
+    swap = [(i, i ^ 1) for i in range(devices)]
     ring = [(i, (i + 1) % devices) for i in range(devices)]
+    factor = 1.0 / math.sqrt(shards * devices * slots * voxels)
+
+    def across_plane(keep, send):
+        parts = pair_sum(count, keep, lax.ppermute(send, "dom", swap))
+        return [parts[0]] + [exchange(parts[step], "dom", step, 2) for step in range(1, count)]
+
+    def finish(streams):
+        parts = plane_sum(streams)
+        parts = [parts[0]] + [exchange(parts[step], "dp", step, 1) for step in range(1, shards)]
+        mine = slab_sum(factor, parts)
+        near = [mine] + [exchange(mine, "dom", step, 2) for step in range(1, count)]
+        return near, [lax.ppermute(value, "dom", swap) for value in near]
+
+    keep_a, keep_b, send_a, send_b = filter_gradient(shards, count, links, own, low, high, pre)
+    stream_a = across_plane(keep_a, send_a)
+    stream_b = across_plane(keep_b, send_b)
+    to_lower, stay, to_upper = input_gradient(
+        links, routes, own, low, high, pre, conv_weight, stream_b[0]
+    )
     from_upper = lax.ppermute(to_lower, "dom", [(b, a) for a, b in ring])
     from_lower = lax.ppermute(to_upper, "dom", ring)
-    conv_keep, conv_send = filter_gradient(shards, where, links, own, low, high, pre)
     fine_grad, down_keep, down_send = fine_gradient(
-        shards, where, from_upper, stay, from_lower, down_weight, fine_act[0]
+        shards, count, from_upper, stay, from_lower, down_weight, fine_act[0]
     )
-
-    count = devices // 2
-    conv_rows, down_rows = conv_keep.shape[1], down_keep.shape[1]
-    piece = -(-(conv_rows + down_rows) // (16 * count)) * 16
-    swap = [(i, i ^ 1) for i in range(devices)]
-    conv_got = lax.ppermute(conv_send, "dom", swap)
-    down_got = lax.ppermute(down_send, "dom", swap)
-    parts = pair_sum(where, count, piece, (conv_keep, down_keep), (conv_got, down_got))
-    parts = [parts[0]] + [exchange(parts[step], "dom", step, 2) for step in range(1, count)]
-    parts = plane_sum(where, parts)
-    parts = [parts[0]] + [exchange(parts[step], "dp", step, 1) for step in range(1, shards)]
-    factor = 1.0 / math.sqrt(shards * devices * slots * voxels)
-    mine = slab_sum(factor, parts)
-    near = [mine] + [exchange(mine, "dom", step, 2) for step in range(1, count)]
-    far = [lax.ppermute(value, "dom", swap) for value in near]
-    conv_grad, down_grad = gather_up(where, conv_rows, down_rows, near, far)
+    stream_d = across_plane(down_keep, down_send)
+    chunk_a = finish([stream_a])
+    chunk_b = finish([stream_b, stream_d])
+    conv_rows = 27 * channels // shards
+    down_rows = down_weight.shape[0] * down_weight.shape[1] // shards
+    piece_a, piece_b, piece_d = (s[0].shape[1] for s in (stream_a, stream_b, stream_d))
+    layout = (((0, 0, piece_a),), ((0, count * piece_a, piece_b), (1, 0, piece_d)))
+    conv_grad, down_grad = gather_up(
+        ((conv_rows, channels), (down_rows, channels)), layout, (chunk_a, chunk_b)
+    )
     return (fine_grad[None], conv_grad, down_grad)
 
 

time: 101 us -> 111 us (1.099)
  starting transfers between devices: 22.6 us -> 33.8 us
  waiting for transfers between devices: 47.1 us -> 38 us
  Pallas kernels: 26.6 us -> 34.6 us
    ppermute x9 -> x21, starting transfers between devices: 11.6 us -> 21.6 us  [exchange(): return lax.ppermute(value, axis, pairs)]
    ppermute x9 -> x21, waiting for transfers between devices: 34.6 us -> 24.7 us  [exchange(): return lax.ppermute(value, axis, pairs)]
    pallas_call x4 -> x7, Pallas kernels: 12.9 us -> 21.3 us  [the longest x1 18.9 us: filter_gradient(): pl.pallas_call(functools.partial(filter_kernel, shard_rows), out_shape=(f...]
    ppermute x6 -> x11, starting transfers between devices: 3.33 us -> 4.43 us  [the longest x3 3.42 us: across_plane(): parts = pair_sum(count, keep, lax.ppermute(send, 'dom', swap))]
    ppermute x6 -> x11, waiting for transfers between devices: 2.87 us -> 3.55 us  [the longest x3 1.91 us: across_plane(): parts = pair_sum(count, keep, lax.ppermute(send, 'dom', swap))]
    unnamed x18 -> x12, local copies, waits for them, and re-layouts: 2.98 us -> 2.97 us
  transfers between devices with their start and end apart: 19 -> 36, of which waited for: 13 -> 17; matrix products, arithmetic and copies ran while one was open for 1% -> 1% of each run, Pallas kernels for 13% -> 13%
where the time goes in v2:
time: 111 us
  waiting for transfers between devices  38 us (34%)
  Pallas kernels  34.6 us (31%)
  starting transfers between devices  33.8 us (30%)
  local copies, waits for them, and re-layouts  3.93 us (4%)
    ppermute x21, waiting for transfers between devices, exchange(): return lax.ppermute(value, axis, pairs)  24.7 us
    ppermute x21, starting transfers between devices, exchange(): return lax.ppermute(value, axis, pairs)  21.6 us
    pallas_call x1, Pallas kernels, filter_gradient(): pl.pallas_call(functools.partial(filter_kernel, shard_rows), out_shape=(f...  18.9 us
    pallas_call x1, Pallas kernels, input_gradient(): pl.pallas_call(input_kernel, out_shape=(out, out, out), in_specs=[SMEM, S...  9.66 us
    ppermute x1, waiting for transfers between devices, body(): from_upper = lax.ppermute(to_lower, 'dom', [(b, a) for a, b in ring])  5.49 us
    ppermute x1, waiting for transfers between devices, body(): from_lower = lax.ppermute(to_upper, 'dom', ring)  3.96 us
    pallas_call x1, Pallas kernels, fine_gradient(): pl.pallas_call(fine_kernel, grid=(3,), out_shape=(jax.ShapeDtypeStruct(fi...  3.55 us
    ppermute x3, starting transfers between devices, across_plane(): parts = pair_sum(count, keep, lax.ppermute(send, 'dom', swap))  3.42 us
  transfers between devices with their start and end apart: 36, of which 17 were waited for; matrix products, arithmetic and copies ran while one was open for 1% of the time, Pallas kernels for 13%

profile of v2, /device:TPU:0, one launch (start us, length us, event | category | flops | bytes accessed | tf_op | source)
XLA Modules:
  0.0 111.0 jit_solution(10714739493298208689)
XLA Ops:
  0.6 1.0 fusion
  1.6 1.3 %collective-permute-start.1 = (bf16[3,64,256]{2,1,0:T(8,128)(2,1)S(1)}, bf16[3,64,256]{2,1,0:T(8,128)(2,1)S(1)}, u32[]{:S(2)}, u32[]{:S(2)}) collective-permute-start(bf16[3,64,256]{2,1,0:T(8,128)(2,1)S(1)} %get-tuple-element.67), channel_id=1, source_target_pairs={{1,0},{2,1},{3,2},{4,3},{5,4},{6,5},{7,6},{9,8},{10,9},{11,10},{12... | collective-permute-start | bytes 294920 | tf_op jit(solution)/shard_map/ppermute | solution.py:519
  2.9 3.0 %collective-permute-start = (bf16[3,64,256]{2,1,0:T(8,128)(2,1)S(1)}, bf16[3,64,256]{2,1,0:T(8,128)(2,1)S(1)}, u32[]{:S(2)}, u32[]{:S(2)}) collective-permute-start(bf16[3,64,256]{2,1,0:T(8,128)(2,1)S(1)} %get-tuple-element.68), channel_id=1, source_target_pairs={{0,1},{1,2},{2,3},{3,4},{4,5},{5,6},{6,7},{8,9},{9,10},{10,11},{11... | collective-permute-start | bytes 294920 | tf_op jit(solution)/shard_map/ppermute | solution.py:518
  5.9 0.7 copy.15
  6.6 0.2 collective-permute-done.low_ref
  6.9 1.1 %copy-done = bf16[1,3,512,256]{3,2,1,0:T(8,128)(2,1)S(1)} copy-done((bf16[1,3,512,256]{3,2,1,0:T(8,128)(2,1)S(1)}, bf16[1,3,512,256]{3,2,1,0:T(8,128)(2,1)}, u32[]{:S(2)}) %copy-start) | copy-done | bytes 786456
  8.0 1.1 %copy-done.2 = bf16[1,3,512,256]{3,2,1,0:T(8,128)(2,1)S(1)} copy-done((bf16[1,3,512,256]{3,2,1,0:T(8,128)(2,1)S(1)}, bf16[1,3,512,256]{3,2,1,0:T(8,128)(2,1)}, u32[]{:S(2)}) %copy-start.2) | copy-done | bytes 786456
  9.1 18.9 %filter_gradient.1 = (bf16[4,896,128]{2,1,0:T(8,128)(2,1)S(1)}, bf16[4,832,128]{2,1,0:T(8,128)(2,1)S(1)}, bf16[4,896,128]{2,1,0:T(8,128)(2,1)S(1)}, bf16[4,832,128]{2,1,0:T(8,128)(2,1)S(1)}) custom-call(s32[3,27]{1,0:T(4,128)S(1)} %bitcast.13, bf16[3,512,256]{2,1,0:T(8,128)(2,1)S(1)} %bitcast.11, bf16[3,64,256]{2,1,0:T(8,128)(2,1)S(1)} %collective-permute-done.low_ref, ...), custom_call_target="tpu_custom_call" | custom-call | flops 5435817984 | bytes 8388608 | tf_op jit(solution)/shard_map/filter_gradient/pallas_call | solution.py:275
  28.1 3.3 %collective-permute-start.2 = (bf16[4,832,128]{2,1,0:T(8,128)(2,1)S(1)}, bf16[4,832,128]{2,1,0:T(8,128)(2,1)S(1)}, u32[]{:S(2)}, u32[]{:S(2)}) collective-permute-start(bf16[4,832,128]{2,1,0:T(8,128)(2,1)S(1)} %get-tuple-element.36), channel_id=1, source_target_pairs={{0,1},{1,0},{2,3},{3,2},{4,5},{5,4},{6,7},{7,6},{8,9},{9,8},{10,11... | collective-permute-start | bytes 2555912 | tf_op jit(solution)/shard_map/ppermute | solution.py:527
  31.4 0.1 collective-permute-start.5
  31.5 1.9 %collective-permute-done.2.got_ref = bf16[4,832,128]{2,1,0:T(8,128)(2,1)S(1)} collective-permute-done((bf16[4,832,128]{2,1,0:T(8,128)(2,1)S(1)}, bf16[4,832,128]{2,1,0:T(8,128)(2,1)S(1)}, u32[]{:S(2)}, u32[]{:S(2)}) %collective-permute-start.2) | collective-permute-done | bytes 852000 | tf_op jit(solution)/shard_map/ppermute | solution.py:527
  33.4 0.2 pair_sum.3
  33.6 0.0 copy-start.1
  33.6 0.0 copy-start.3
  33.6 9.7 %input_gradient.1 = (bf16[1,512,256]{2,1,0:T(8,128)(2,1)S(1)}, bf16[1,512,256]{2,1,0:T(8,128)(2,1)S(1)}, bf16[1,512,256]{2,1,0:T(8,128)(2,1)S(1)}) custom-call(s32[3,27]{1,0:T(4,128)S(1)} %bitcast.14, s32[3,8]{1,0:T(4,128)S(1)} %bitcast.15, bf16[3,512,256]{2,1,0:T(8,128)(2,1)S(1)} %bitcast.12, bf16[3,64,256]{2,1,0:T(8,128)(2,1)S(1)} %collective-permute-done.low_ref, ...), custom_call_target="tpu_custom_call" | custom-call | flops 5435817984 | bytes 8388608 | tf_op jit(solution)/shard_map/input_gradient/pallas_call | solution.py:190
  43.3 3.4 %collective-permute-start.3 = (bf16[1,512,256]{2,1,0:T(8,128)(2,1)S(1)}, bf16[1,512,256]{2,1,0:T(8,128)(2,1)S(1)}, u32[]{:S(2)}, u32[]{:S(2)}) collective-permute-start(bf16[1,512,256]{2,1,0:T(8,128)(2,1)S(1)} %get-tuple-element.38), channel_id=1, source_target_pairs={{1,0},{2,1},{3,2},{4,3},{5,4},{6,5},{7,6},{0,7},{9,8},{10,9},{11,1... | collective-permute-start | bytes 786440 | tf_op jit(solution)/shard_map/ppermute | solution.py:543
  46.7 5.5 %collective-permute-done.3.upper_ref = bf16[1,512,256]{2,1,0:T(8,128)(2,1)S(1)} collective-permute-done((bf16[1,512,256]{2,1,0:T(8,128)(2,1)S(1)}, bf16[1,512,256]{2,1,0:T(8,128)(2,1)S(1)}, u32[]{:S(2)}, u32[]{:S(2)}) %collective-permute-start.3) | collective-permute-done | bytes 262176 | tf_op jit(solution)/shard_map/ppermute | solution.py:543
  52.2 4.0 %collective-permute-done.4.lower_ref = bf16[1,512,256]{2,1,0:T(8,128)(2,1)S(1)} collective-permute-done((bf16[1,512,256]{2,1,0:T(8,128)(2,1)S(1)}, bf16[1,512,256]{2,1,0:T(8,128)(2,1)S(1)}, u32[]{:S(2)}, u32[]{:S(2)}) %collective-permute-start.4) | collective-permute-done | bytes 262176 | tf_op jit(solution)/shard_map/ppermute | solution.py:544
  56.2 3.5 %fine_gradient.1 = (bf16[24,512,128]{2,1,0:T(8,128)(2,1)}, bf16[4,256,128]{2,1,0:T(8,128)(2,1)S(1)}, bf16[4,256,128]{2,1,0:T(8,128)(2,1)S(1)}) custom-call(bf16[1,512,256]{2,1,0:T(8,128)(2,1)S(1)} %collective-permute-done.3.upper_ref, bf16[1,512,256]{2,1,0:T(8,128)(2,1)S(1)} %get-tuple-element.39.stay_ref, ...), custom_call_target="tpu_custom_call" | custom-call | flops 1610612736 | bytes 8388608 | tf_op jit(solution)/shard_map/fine_gradient/pallas_call | solution.py:361
  59.7 0.0 collective-permute-start.22
  59.7 0.0 collective-permute-start.19
  59.7 0.0 collective-permute-done.5.got_ref
  59.7 0.3 pair_sum.4
  60.0 2.1 %collective-permute-start.6 = (bf16[4,224,128]{2,1,0:T(8,128)(2,1)S(1)}, bf16[4,224,128]{2,1,0:T(8,128)(2,1)S(1)}, u32[]{:S(2)}, u32[]{:S(2)}) collective-permute-start(bf16[4,224,128]{2,1,0:T(8,128)(2,1)S(1)} %get-tuple-element.45), channel_id=1, source_target_pairs={{0,2},{1,3},{2,0},{3,1},{4,6},{5,7},{6,4},{7,5},{8,10},{9,11},{10,... | collective-permute-start | bytes 688136 | tf_op jit(solution)/shard_map/ppermute | solution.py:46
  62.0 0.4 collective-permute-start.7
  62.4 1.2 %collective-permute-start.8 = (bf16[4,224,128]{2,1,0:T(8,128)(2,1)S(1)}, bf16[4,224,128]{2,1,0:T(8,128)(2,1)S(1)}, u32[]{:S(2)}, u32[]{:S(2)}) collective-permute-start(bf16[4,224,128]{2,1,0:T(8,128)(2,1)S(1)} %get-tuple-element.47), channel_id=1, source_target_pairs={{0,6},{1,7},{2,4},{3,5},{4,2},{5,3},{6,0},{7,1},{8,14},{9,15},{10,... | collective-permute-start | bytes 688136 | tf_op jit(solution)/shard_map/ppermute | solution.py:46
  63.6 4.2 %collective-permute-done.19.refs_1_ = bf16[4,208,128]{2,1,0:T(8,128)(2,1)S(1)} collective-permute-done((bf16[4,208,128]{2,1,0:T(8,128)(2,1)S(1)}, bf16[4,208,128]{2,1,0:T(8,128)(2,1)S(1)}, u32[]{:S(2)}, u32[]{:S(2)}) %collective-permute-start.19) | collective-permute-done | bytes 213024 | tf_op jit(solution)/shard_map/ppermute | solution.py:46
  67.8 0.4 collective-permute-start.20
  68.2 1.1 %collective-permute-start.21 = (bf16[4,208,128]{2,1,0:T(8,128)(2,1)S(1)}, bf16[4,208,128]{2,1,0:T(8,128)(2,1)S(1)}, u32[]{:S(2)}, u32[]{:S(2)}) collective-permute-start(bf16[4,208,128]{2,1,0:T(8,128)(2,1)S(1)} %get-tuple-element.54), channel_id=1, source_target_pairs={{0,6},{1,7},{2,4},{3,5},{4,2},{5,3},{6,0},{7,1},{8,14},{9,15},{10,... | collective-permute-start | bytes 638984 | tf_op jit(solution)/shard_map/ppermute | solution.py:46
  69.3 0.1 pair_sum.5
  69.4 3.3 %collective-permute-done.6.refs_1_ = bf16[4,224,128]{2,1,0:T(8,128)(2,1)S(1)} collective-permute-done((bf16[4,224,128]{2,1,0:T(8,128)(2,1)S(1)}, bf16[4,224,128]{2,1,0:T(8,128)(2,1)S(1)}, u32[]{:S(2)}, u32[]{:S(2)}) %collective-permute-start.6) | collective-permute-done | bytes 229408 | tf_op jit(solution)/shard_map/ppermute | solution.py:46
  72.7 0.1 collective-permute-start.23
  72.8 0.7 collective-permute-start.24
  73.5 4.1 %collective-permute-done.8.refs_3_ = bf16[4,224,128]{2,1,0:T(8,128)(2,1)S(1)} collective-permute-done((bf16[4,224,128]{2,1,0:T(8,128)(2,1)S(1)}, bf16[4,224,128]{2,1,0:T(8,128)(2,1)S(1)}, u32[]{:S(2)}, u32[]{:S(2)}) %collective-permute-start.8) | collective-permute-done | bytes 229408 | tf_op jit(solution)/shard_map/ppermute | solution.py:46
  77.6 1.1 %collective-permute-start.25 = (bf16[4,64,128]{2,1,0:T(8,128)(2,1)S(1)}, bf16[4,64,128]{2,1,0:T(8,128)(2,1)S(1)}, u32[]{:S(2)}, u32[]{:S(2)}) collective-permute-start(bf16[4,64,128]{2,1,0:T(8,128)(2,1)S(1)} %get-tuple-element.60), channel_id=1, source_target_pairs={{0,6},{1,7},{2,4},{3,5},{4,2},{5,3},{6,0},{7,1},{8,14},{9,15},{10,... | collective-permute-start | bytes 196616 | tf_op jit(solution)/shard_map/ppermute | solution.py:46
  78.7 0.1 plane_sum.2
  78.8 7.1 %collective-permute-done.20.refs_2_ = bf16[4,208,128]{2,1,0:T(8,128)(2,1)S(1)} collective-permute-done((bf16[4,208,128]{2,1,0:T(8,128)(2,1)S(1)}, bf16[4,208,128]{2,1,0:T(8,128)(2,1)S(1)}, u32[]{:S(2)}, u32[]{:S(2)}) %collective-permute-start.20) | collective-permute-done | bytes 213024 | tf_op jit(solution)/shard_map/ppermute | solution.py:46
  85.9 1.6 %collective-permute-start.9 = (bf16[224,128]{1,0:T(8,128)(2,1)S(1)}, bf16[224,128]{1,0:T(8,128)(2,1)S(1)}, u32[]{:S(2)}, u32[]{:S(2)}) collective-permute-start(bf16[224,128]{1,0:T(8,128)(2,1)S(1)} %get-tuple-element.49), channel_id=1, source_target_pairs={{0,8},{8,0},{16,24},{24,16},{1,9},{9,1},{17,25},{25,17},{2,10},{10... | collective-permute-start | bytes 172040 | tf_op jit(solution)/shard_map/ppermute | solution.py:46
  87.4 2.6 %collective-permute-start.10 = (bf16[224,128]{1,0:T(8,128)(2,1)S(1)}, bf16[224,128]{1,0:T(8,128)(2,1)S(1)}, u32[]{:S(2)}, u32[]{:S(2)}) collective-permute-start(bf16[224,128]{1,0:T(8,128)(2,1)S(1)} %get-tuple-element.50), channel_id=1, source_target_pairs={{0,16},{8,24},{16,0},{24,8},{1,17},{9,25},{17,1},{25,9},{2,18},{10... | collective-permute-start | bytes 172040 | tf_op jit(solution)/shard_map/ppermute | solution.py:46
  90.0 0.1 plane_sum.3
  90.2 0.5 collective-permute-start.26
  90.7 1.4 %collective-permute-start.11 = (bf16[224,128]{1,0:T(8,128)(2,1)S(1)}, bf16[224,128]{1,0:T(8,128)(2,1)S(1)}, u32[]{:S(2)}, u32[]{:S(2)}) collective-permute-start(bf16[224,128]{1,0:T(8,128)(2,1)S(1)} %get-tuple-element.51), channel_id=1, source_target_pairs={{0,24},{8,16},{16,8},{24,0},{1,25},{9,17},{17,9},{25,1},{2,26},{10... | collective-permute-start | bytes 172040 | tf_op jit(solution)/shard_map/ppermute | solution.py:46
  92.0 1.7 %collective-permute-start.27 = (bf16[272,128]{1,0:T(8,128)(2,1)S(1)}, bf16[272,128]{1,0:T(8,128)(2,1)S(1)}, u32[]{:S(2)}, u32[]{:S(2)}) collective-permute-start(bf16[272,128]{1,0:T(8,128)(2,1)S(1)} %get-tuple-element.63), channel_id=1, source_target_pairs={{0,16},{8,24},{16,0},{24,8},{1,17},{9,25},{17,1},{25,9},{2,18},{10... | collective-permute-start | bytes 208904 | tf_op jit(solution)/shard_map/ppermute | solution.py:46
  93.7 0.9 collective-permute-start.28
  94.6 0.3 collective-permute-done.10.refs_2_
  95.0 1.7 %collective-permute-done.11.refs_3_ = bf16[224,128]{1,0:T(8,128)(2,1)S(1)} collective-permute-done((bf16[224,128]{1,0:T(8,128)(2,1)S(1)}, bf16[224,128]{1,0:T(8,128)(2,1)S(1)}, u32[]{:S(2)}, u32[]{:S(2)}) %collective-permute-start.11) | collective-permute-done | bytes 57376 | tf_op jit(solution)/shard_map/ppermute | solution.py:46
  96.8 0.1 collective-permute-start.15
  96.8 0.3 collective-permute-start.14
  97.2 1.7 %collective-permute-start.13 = (bf16[224,128]{1,0:T(8,128)(2,1)S(1)}, bf16[224,128]{1,0:T(8,128)(2,1)S(1)}, u32[]{:S(2)}, u32[]{:S(2)}) collective-permute-start(bf16[224,128]{1,0:T(8,128)(2,1)S(1)} %slab_sum.2.refs_0_), channel_id=1, source_target_pairs={{0,4},{1,5},{2,6},{3,7},{4,0},{5,1},{6,2},{7,3},{8,12},{9,13},{10,... | collective-permute-start | bytes 172040 | tf_op jit(solution)/shard_map/ppermute | solution.py:46
  98.9 1.2 %collective-permute-done.27.refs_2_ = bf16[272,128]{1,0:T(8,128)(2,1)S(1)} collective-permute-done((bf16[272,128]{1,0:T(8,128)(2,1)S(1)}, bf16[272,128]{1,0:T(8,128)(2,1)S(1)}, u32[]{:S(2)}, u32[]{:S(2)}) %collective-permute-start.27) | collective-permute-done | bytes 69664 | tf_op jit(solution)/shard_map/ppermute | solution.py:46
  100.1 0.3 collective-permute-start.12
  100.4 1.3 %collective-permute-start.31 = (bf16[272,128]{1,0:T(8,128)(2,1)S(1)}, bf16[272,128]{1,0:T(8,128)(2,1)S(1)}, u32[]{:S(2)}, u32[]{:S(2)}) collective-permute-start(bf16[272,128]{1,0:T(8,128)(2,1)S(1)} %slab_sum.3.refs_8_), channel_id=1, source_target_pairs={{0,6},{1,7},{2,4},{3,5},{4,2},{5,3},{6,0},{7,1},{8,14},{9,15},{10,... | collective-permute-start | bytes 208904 | tf_op jit(solution)/shard_map/ppermute | solution.py:46
  101.8 1.9 %collective-permute-start.30 = (bf16[272,128]{1,0:T(8,128)(2,1)S(1)}, bf16[272,128]{1,0:T(8,128)(2,1)S(1)}, u32[]{:S(2)}, u32[]{:S(2)}) collective-permute-start(bf16[272,128]{1,0:T(8,128)(2,1)S(1)} %slab_sum.3.refs_8_), channel_id=1, source_target_pairs={{0,4},{1,5},{2,6},{3,7},{4,0},{5,1},{6,2},{7,3},{8,12},{9,13},{10,... | collective-permute-start | bytes 208904 | tf_op jit(solution)/shard_map/ppermute | solution.py:46
  103.7 0.3 collective-permute-start.29
  104.0 0.2 collective-permute-done.12.refs_1_
  104.3 0.3 collective-permute-start.17
  104.5 0.7 collective-permute-done.18.refs_7_
  105.3 0.2 collective-permute-start.32
  105.4 0.7 collective-permute-done.31.refs_11_
  106.1 0.5 collective-permute-done.30.refs_10_
  106.7 1.3 %collective-permute-done.29.refs_9_ = bf16[272,128]{1,0:T(8,128)(2,1)S(1)} collective-permute-done((bf16[272,128]{1,0:T(8,128)(2,1)S(1)}, bf16[272,128]{1,0:T(8,128)(2,1)S(1)}, u32[]{:S(2)}, u32[]{:S(2)}) %collective-permute-start.29) | collective-permute-done | bytes 69664 | tf_op jit(solution)/shard_map/ppermute | solution.py:46
  108.0 0.5 collective-permute-start.16
  108.5 0.9 collective-permute-done.16.refs_5_
  109.4 1.6 %gather_up.1 = (f32[1728,256]{1,0:T(8,128)}, f32[256,256]{1,0:T(8,128)}) custom-call(bf16[224,128]{1,0:T(8,128)(2,1)S(1)} %slab_sum.2.refs_0_, bf16[224,128]{1,0:T(8,128)(2,1)S(1)} %collective-permute-done.12.refs_1_, bf16[224,128]{1,0:T(8,128)(2,1)S(1)} %collective-permute-done.13.refs_2_, bf16[224,128]{1,0:T(8,128)(2,1)S(1)} %collective-permute-done.14.refs_3_, ...), custom_call_target="tpu_custom_call" | custom-call | flops 3047424 | bytes 3047424 | tf_op jit(solution)/shard_map/gather_up/pallas_call | solution.py:491
  (32 shorter events, 0.2 us)
Async XLA Ops:
  1.6 5.0 %collective-permute-start.1 = (bf16[3,64,256]{2,1,0:T(8,128)(2,1)S(1)}, bf16[3,64,256]{2,1,0:T(8,128)(2,1)S(1)}, u32[]{:S(2)}, u32[]{:S(2)}) collective-permute-start(bf16[3,64,256]{2,1,0:T(8,128)(2,1)S(1)} %get-tuple-element.67), channel_id=1, source_target_pairs={{1,0},{2,1},{3,2},{4,3},{5,4},{6,5},{7,6},{9,8},{10,9},{11,10},{12... | collective-permute-start | bytes 294920 | tf_op jit(solution)/shard_map/ppermute | solution.py:519
  2.9 4.0 %collective-permute-start = (bf16[3,64,256]{2,1,0:T(8,128)(2,1)S(1)}, bf16[3,64,256]{2,1,0:T(8,128)(2,1)S(1)}, u32[]{:S(2)}, u32[]{:S(2)}) collective-permute-start(bf16[3,64,256]{2,1,0:T(8,128)(2,1)S(1)} %get-tuple-element.68), channel_id=1, source_target_pairs={{0,1},{1,2},{2,3},{3,4},{4,5},{5,6},{6,7},{8,9},{9,10},{10,11},{11... | collective-permute-start | bytes 294920 | tf_op jit(solution)/shard_map/ppermute | solution.py:518
  6.9 1.1 %copy-start = (bf16[1,3,512,256]{3,2,1,0:T(8,128)(2,1)S(1)}, bf16[1,3,512,256]{3,2,1,0:T(8,128)(2,1)}, u32[]{:S(2)}) copy-start(bf16[1,3,512,256]{3,2,1,0:T(8,128)(2,1)} %param.7) | copy-start | bytes 2359300
  8.0 1.1 %copy-start.2 = (bf16[1,3,512,256]{3,2,1,0:T(8,128)(2,1)S(1)}, bf16[1,3,512,256]{3,2,1,0:T(8,128)(2,1)}, u32[]{:S(2)}) copy-start(bf16[1,3,512,256]{3,2,1,0:T(8,128)(2,1)} %param.8) | copy-start | bytes 2359300
  9.1 22.3 %copy-start.4 = (s32[1,1,3,8]{3,1,2,0:T(1,128)S(1)}, s32[1,1,3,8]{3,1,2,0:T(1,128)}, u32[]{:S(2)}) copy-start(s32[1,1,3,8]{3,1,2,0:T(1,128)} %param.13) | copy-start | bytes 292
  28.1 5.3 %collective-permute-start.2 = (bf16[4,832,128]{2,1,0:T(8,128)(2,1)S(1)}, bf16[4,832,128]{2,1,0:T(8,128)(2,1)S(1)}, u32[]{:S(2)}, u32[]{:S(2)}) collective-permute-start(bf16[4,832,128]{2,1,0:T(8,128)(2,1)S(1)} %get-tuple-element.36), channel_id=1, source_target_pairs={{0,1},{1,0},{2,3},{3,2},{4,5},{5,4},{6,7},{7,6},{8,9},{9,8},{10,11... | collective-permute-start | bytes 2555912 | tf_op jit(solution)/shard_map/ppermute | solution.py:527
  31.4 28.3 %collective-permute-start.5 = (bf16[4,896,128]{2,1,0:T(8,128)(2,1)S(1)}, bf16[4,896,128]{2,1,0:T(8,128)(2,1)S(1)}, u32[]{:S(2)}, u32[]{:S(2)}) collective-permute-start(bf16[4,896,128]{2,1,0:T(8,128)(2,1)S(1)} %get-tuple-element.43), channel_id=1, source_target_pairs={{0,1},{1,0},{2,3},{3,2},{4,5},{5,4},{6,7},{7,6},{8,9},{9,8},{10,11... | collective-permute-start | bytes 2752520 | tf_op jit(solution)/shard_map/ppermute | solution.py:527
  33.6 22.6 %copy-start.1 = (bf16[1,24,512,128]{3,2,1,0:T(8,128)(2,1)S(1)}, bf16[1,24,512,128]{3,2,1,0:T(8,128)(2,1)}, u32[]{:S(2)}) copy-start(bf16[1,24,512,128]{3,2,1,0:T(8,128)(2,1)} %param.11) | copy-start | bytes 9437188
  33.6 22.6 %copy-start.3 = (bf16[8,128,256]{2,1,0:T(8,128)(2,1)S(1)}, bf16[8,128,256]{2,1,0:T(8,128)(2,1)}, u32[]{:S(2)}) copy-start(bf16[8,128,256]{2,1,0:T(8,128)(2,1)} %weight_ref.3) | copy-start | bytes 1572868
  43.3 8.9 %collective-permute-start.3 = (bf16[1,512,256]{2,1,0:T(8,128)(2,1)S(1)}, bf16[1,512,256]{2,1,0:T(8,128)(2,1)S(1)}, u32[]{:S(2)}, u32[]{:S(2)}) collective-permute-start(bf16[1,512,256]{2,1,0:T(8,128)(2,1)S(1)} %get-tuple-element.38), channel_id=1, source_target_pairs={{1,0},{2,1},{3,2},{4,3},{5,4},{6,5},{7,6},{0,7},{9,8},{10,9},{11,1... | collective-permute-start | bytes 786440 | tf_op jit(solution)/shard_map/ppermute | solution.py:543
  46.7 9.5 %collective-permute-start.4 = (bf16[1,512,256]{2,1,0:T(8,128)(2,1)S(1)}, bf16[1,512,256]{2,1,0:T(8,128)(2,1)S(1)}, u32[]{:S(2)}, u32[]{:S(2)}) collective-permute-start(bf16[1,512,256]{2,1,0:T(8,128)(2,1)S(1)} %get-tuple-element.40), channel_id=1, source_target_pairs={{0,1},{1,2},{2,3},{3,4},{4,5},{5,6},{6,7},{7,0},{8,9},{9,10},{10,1... | collective-permute-start | bytes 786440 | tf_op jit(solution)/shard_map/ppermute | solution.py:544
  59.7 8.5 %collective-permute-start.22 = (bf16[4,256,128]{2,1,0:T(8,128)(2,1)S(1)}, bf16[4,256,128]{2,1,0:T(8,128)(2,1)S(1)}, u32[]{:S(2)}, u32[]{:S(2)}) collective-permute-start(bf16[4,256,128]{2,1,0:T(8,128)(2,1)S(1)} %get-tuple-element.56), channel_id=1, source_target_pairs={{0,1},{1,0},{2,3},{3,2},{4,5},{5,4},{6,7},{7,6},{8,9},{9,8},{10,11... | collective-permute-start | bytes 786440 | tf_op jit(solution)/shard_map/ppermute | solution.py:527
  59.7 8.0 %collective-permute-start.19 = (bf16[4,208,128]{2,1,0:T(8,128)(2,1)S(1)}, bf16[4,208,128]{2,1,0:T(8,128)(2,1)S(1)}, u32[]{:S(2)}, u32[]{:S(2)}) collective-permute-start(bf16[4,208,128]{2,1,0:T(8,128)(2,1)S(1)} %get-tuple-element.52), channel_id=1, source_target_pairs={{0,2},{1,3},{2,0},{3,1},{4,6},{5,7},{6,4},{7,5},{8,10},{9,11},{10,... | collective-permute-start | bytes 638984 | tf_op jit(solution)/shard_map/ppermute | solution.py:46
  60.0 12.7 %collective-permute-start.6 = (bf16[4,224,128]{2,1,0:T(8,128)(2,1)S(1)}, bf16[4,224,128]{2,1,0:T(8,128)(2,1)S(1)}, u32[]{:S(2)}, u32[]{:S(2)}) collective-permute-start(bf16[4,224,128]{2,1,0:T(8,128)(2,1)S(1)} %get-tuple-element.45), channel_id=1, source_target_pairs={{0,2},{1,3},{2,0},{3,1},{4,6},{5,7},{6,4},{7,5},{8,10},{9,11},{10,... | collective-permute-start | bytes 688136 | tf_op jit(solution)/shard_map/ppermute | solution.py:46
  62.0 10.7 %collective-permute-start.7 = (bf16[4,224,128]{2,1,0:T(8,128)(2,1)S(1)}, bf16[4,224,128]{2,1,0:T(8,128)(2,1)S(1)}, u32[]{:S(2)}, u32[]{:S(2)}) collective-permute-start(bf16[4,224,128]{2,1,0:T(8,128)(2,1)S(1)} %get-tuple-element.46), channel_id=1, source_target_pairs={{0,4},{1,5},{2,6},{3,7},{4,0},{5,1},{6,2},{7,3},{8,12},{9,13},{10,... | collective-permute-start | bytes 688136 | tf_op jit(solution)/shard_map/ppermute | solution.py:46
  62.4 15.2 %collective-permute-start.8 = (bf16[4,224,128]{2,1,0:T(8,128)(2,1)S(1)}, bf16[4,224,128]{2,1,0:T(8,128)(2,1)S(1)}, u32[]{:S(2)}, u32[]{:S(2)}) collective-permute-start(bf16[4,224,128]{2,1,0:T(8,128)(2,1)S(1)} %get-tuple-element.47), channel_id=1, source_target_pairs={{0,6},{1,7},{2,4},{3,5},{4,2},{5,3},{6,0},{7,1},{8,14},{9,15},{10,... | collective-permute-start | bytes 688136 | tf_op jit(solution)/shard_map/ppermute | solution.py:46
  67.8 18.1 %collective-permute-start.20 = (bf16[4,208,128]{2,1,0:T(8,128)(2,1)S(1)}, bf16[4,208,128]{2,1,0:T(8,128)(2,1)S(1)}, u32[]{:S(2)}, u32[]{:S(2)}) collective-permute-start(bf16[4,208,128]{2,1,0:T(8,128)(2,1)S(1)} %get-tuple-element.53), channel_id=1, source_target_pairs={{0,4},{1,5},{2,6},{3,7},{4,0},{5,1},{6,2},{7,3},{8,12},{9,13},{10,... | collective-permute-start | bytes 638984 | tf_op jit(solution)/shard_map/ppermute | solution.py:46
  68.2 19.2 %collective-permute-start.21 = (bf16[4,208,128]{2,1,0:T(8,128)(2,1)S(1)}, bf16[4,208,128]{2,1,0:T(8,128)(2,1)S(1)}, u32[]{:S(2)}, u32[]{:S(2)}) collective-permute-start(bf16[4,208,128]{2,1,0:T(8,128)(2,1)S(1)} %get-tuple-element.54), channel_id=1, source_target_pairs={{0,6},{1,7},{2,4},{3,5},{4,2},{5,3},{6,0},{7,1},{8,14},{9,15},{10,... | collective-permute-start | bytes 638984 | tf_op jit(solution)/shard_map/ppermute | solution.py:46
  72.7 17.3 %collective-permute-start.23 = (bf16[4,64,128]{2,1,0:T(8,128)(2,1)S(1)}, bf16[4,64,128]{2,1,0:T(8,128)(2,1)S(1)}, u32[]{:S(2)}, u32[]{:S(2)}) collective-permute-start(bf16[4,64,128]{2,1,0:T(8,128)(2,1)S(1)} %get-tuple-element.58), channel_id=1, source_target_pairs={{0,2},{1,3},{2,0},{3,1},{4,6},{5,7},{6,4},{7,5},{8,10},{9,11},{10,... | collective-permute-start | bytes 196616 | tf_op jit(solution)/shard_map/ppermute | solution.py:46
  72.8 17.3 %collective-permute-start.24 = (bf16[4,64,128]{2,1,0:T(8,128)(2,1)S(1)}, bf16[4,64,128]{2,1,0:T(8,128)(2,1)S(1)}, u32[]{:S(2)}, u32[]{:S(2)}) collective-permute-start(bf16[4,64,128]{2,1,0:T(8,128)(2,1)S(1)} %get-tuple-element.59), channel_id=1, source_target_pairs={{0,4},{1,5},{2,6},{3,7},{4,0},{5,1},{6,2},{7,3},{8,12},{9,13},{10,... | collective-permute-start | bytes 196616 | tf_op jit(solution)/shard_map/ppermute | solution.py:46
  77.6 12.5 %collective-permute-start.25 = (bf16[4,64,128]{2,1,0:T(8,128)(2,1)S(1)}, bf16[4,64,128]{2,1,0:T(8,128)(2,1)S(1)}, u32[]{:S(2)}, u32[]{:S(2)}) collective-permute-start(bf16[4,64,128]{2,1,0:T(8,128)(2,1)S(1)} %get-tuple-element.60), channel_id=1, source_target_pairs={{0,6},{1,7},{2,4},{3,5},{4,2},{5,3},{6,0},{7,1},{8,14},{9,15},{10,... | collective-permute-start | bytes 196616 | tf_op jit(solution)/shard_map/ppermute | solution.py:46
  85.9 7.9 %collective-permute-start.9 = (bf16[224,128]{1,0:T(8,128)(2,1)S(1)}, bf16[224,128]{1,0:T(8,128)(2,1)S(1)}, u32[]{:S(2)}, u32[]{:S(2)}) collective-permute-start(bf16[224,128]{1,0:T(8,128)(2,1)S(1)} %get-tuple-element.49), channel_id=1, source_target_pairs={{0,8},{8,0},{16,24},{24,16},{1,9},{9,1},{17,25},{25,17},{2,10},{10... | collective-permute-start | bytes 172040 | tf_op jit(solution)/shard_map/ppermute | solution.py:46
  87.4 7.6 %collective-permute-start.10 = (bf16[224,128]{1,0:T(8,128)(2,1)S(1)}, bf16[224,128]{1,0:T(8,128)(2,1)S(1)}, u32[]{:S(2)}, u32[]{:S(2)}) collective-permute-start(bf16[224,128]{1,0:T(8,128)(2,1)S(1)} %get-tuple-element.50), channel_id=1, source_target_pairs={{0,16},{8,24},{16,0},{24,8},{1,17},{9,25},{17,1},{25,9},{2,18},{10... | collective-permute-start | bytes 172040 | tf_op jit(solution)/shard_map/ppermute | solution.py:46
  90.2 7.0 %collective-permute-start.26 = (bf16[272,128]{1,0:T(8,128)(2,1)S(1)}, bf16[272,128]{1,0:T(8,128)(2,1)S(1)}, u32[]{:S(2)}, u32[]{:S(2)}) collective-permute-start(bf16[272,128]{1,0:T(8,128)(2,1)S(1)} %get-tuple-element.62), channel_id=1, source_target_pairs={{0,8},{8,0},{16,24},{24,16},{1,9},{9,1},{17,25},{25,17},{2,10},{10... | collective-permute-start | bytes 208904 | tf_op jit(solution)/shard_map/ppermute | solution.py:46
  90.7 6.0 %collective-permute-start.11 = (bf16[224,128]{1,0:T(8,128)(2,1)S(1)}, bf16[224,128]{1,0:T(8,128)(2,1)S(1)}, u32[]{:S(2)}, u32[]{:S(2)}) collective-permute-start(bf16[224,128]{1,0:T(8,128)(2,1)S(1)} %get-tuple-element.51), channel_id=1, source_target_pairs={{0,24},{8,16},{16,8},{24,0},{1,25},{9,17},{17,9},{25,1},{2,26},{10... | collective-permute-start | bytes 172040 | tf_op jit(solution)/shard_map/ppermute | solution.py:46
  92.0 8.0 %collective-permute-start.27 = (bf16[272,128]{1,0:T(8,128)(2,1)S(1)}, bf16[272,128]{1,0:T(8,128)(2,1)S(1)}, u32[]{:S(2)}, u32[]{:S(2)}) collective-permute-start(bf16[272,128]{1,0:T(8,128)(2,1)S(1)} %get-tuple-element.63), channel_id=1, source_target_pairs={{0,16},{8,24},{16,0},{24,8},{1,17},{9,25},{17,1},{25,9},{2,18},{10... | collective-permute-start | bytes 208904 | tf_op jit(solution)/shard_map/ppermute | solution.py:46
  93.7 6.7 %collective-permute-start.28 = (bf16[272,128]{1,0:T(8,128)(2,1)S(1)}, bf16[272,128]{1,0:T(8,128)(2,1)S(1)}, u32[]{:S(2)}, u32[]{:S(2)}) collective-permute-start(bf16[272,128]{1,0:T(8,128)(2,1)S(1)} %get-tuple-element.64), channel_id=1, source_target_pairs={{0,24},{8,16},{16,8},{24,0},{1,25},{9,17},{17,9},{25,1},{2,26},{10... | collective-permute-start | bytes 208904 | tf_op jit(solution)/shard_map/ppermute | solution.py:46
  96.8 5.0 %collective-permute-start.15 = (bf16[224,128]{1,0:T(8,128)(2,1)S(1)}, bf16[224,128]{1,0:T(8,128)(2,1)S(1)}, u32[]{:S(2)}, u32[]{:S(2)}) collective-permute-start(bf16[224,128]{1,0:T(8,128)(2,1)S(1)} %slab_sum.2.refs_0_), channel_id=1, source_target_pairs={{0,1},{1,0},{2,3},{3,2},{4,5},{5,4},{6,7},{7,6},{8,9},{9,8},{10,11... | collective-permute-start | bytes 172040 | tf_op jit(solution)/shard_map/ppermute | solution.py:535
  96.8 6.9 %collective-permute-start.14 = (bf16[224,128]{1,0:T(8,128)(2,1)S(1)}, bf16[224,128]{1,0:T(8,128)(2,1)S(1)}, u32[]{:S(2)}, u32[]{:S(2)}) collective-permute-start(bf16[224,128]{1,0:T(8,128)(2,1)S(1)} %slab_sum.2.refs_0_), channel_id=1, source_target_pairs={{0,6},{1,7},{2,4},{3,5},{4,2},{5,3},{6,0},{7,1},{8,14},{9,15},{10,... | collective-permute-start | bytes 172040 | tf_op jit(solution)/shard_map/ppermute | solution.py:46
  97.2 6.9 %collective-permute-start.13 = (bf16[224,128]{1,0:T(8,128)(2,1)S(1)}, bf16[224,128]{1,0:T(8,128)(2,1)S(1)}, u32[]{:S(2)}, u32[]{:S(2)}) collective-permute-start(bf16[224,128]{1,0:T(8,128)(2,1)S(1)} %slab_sum.2.refs_0_), channel_id=1, source_target_pairs={{0,4},{1,5},{2,6},{3,7},{4,0},{5,1},{6,2},{7,3},{8,12},{9,13},{10,... | collective-permute-start | bytes 172040 | tf_op jit(solution)/shard_map/ppermute | solution.py:46
  100.1 4.2 %collective-permute-start.12 = (bf16[224,128]{1,0:T(8,128)(2,1)S(1)}, bf16[224,128]{1,0:T(8,128)(2,1)S(1)}, u32[]{:S(2)}, u32[]{:S(2)}) collective-permute-start(bf16[224,128]{1,0:T(8,128)(2,1)S(1)} %slab_sum.2.refs_0_), channel_id=1, source_target_pairs={{0,2},{1,3},{2,0},{3,1},{4,6},{5,7},{6,4},{7,5},{8,10},{9,11},{10,... | collective-permute-start | bytes 172040 | tf_op jit(solution)/shard_map/ppermute | solution.py:46
  100.4 5.7 %collective-permute-start.31 = (bf16[272,128]{1,0:T(8,128)(2,1)S(1)}, bf16[272,128]{1,0:T(8,128)(2,1)S(1)}, u32[]{:S(2)}, u32[]{:S(2)}) collective-permute-start(bf16[272,128]{1,0:T(8,128)(2,1)S(1)} %slab_sum.3.refs_8_), channel_id=1, source_target_pairs={{0,6},{1,7},{2,4},{3,5},{4,2},{5,3},{6,0},{7,1},{8,14},{9,15},{10,... | collective-permute-start | bytes 208904 | tf_op jit(solution)/shard_map/ppermute | solution.py:46
  101.8 4.9 %collective-permute-start.30 = (bf16[272,128]{1,0:T(8,128)(2,1)S(1)}, bf16[272,128]{1,0:T(8,128)(2,1)S(1)}, u32[]{:S(2)}, u32[]{:S(2)}) collective-permute-start(bf16[272,128]{1,0:T(8,128)(2,1)S(1)} %slab_sum.3.refs_8_), channel_id=1, source_target_pairs={{0,4},{1,5},{2,6},{3,7},{4,0},{5,1},{6,2},{7,3},{8,12},{9,13},{10,... | collective-permute-start | bytes 208904 | tf_op jit(solution)/shard_map/ppermute | solution.py:46
  103.7 4.3 %collective-permute-start.29 = (bf16[272,128]{1,0:T(8,128)(2,1)S(1)}, bf16[272,128]{1,0:T(8,128)(2,1)S(1)}, u32[]{:S(2)}, u32[]{:S(2)}) collective-permute-start(bf16[272,128]{1,0:T(8,128)(2,1)S(1)} %slab_sum.3.refs_8_), channel_id=1, source_target_pairs={{0,2},{1,3},{2,0},{3,1},{4,6},{5,7},{6,4},{7,5},{8,10},{9,11},{10,... | collective-permute-start | bytes 208904 | tf_op jit(solution)/shard_map/ppermute | solution.py:46
  104.0 1.2 %collective-permute-start.18 = (bf16[224,128]{1,0:T(8,128)(2,1)S(1)}, bf16[224,128]{1,0:T(8,128)(2,1)S(1)}, u32[]{:S(2)}, u32[]{:S(2)}) collective-permute-start(bf16[224,128]{1,0:T(8,128)(2,1)S(1)} %collective-permute-done.14.refs_3_), channel_id=1, source_target_pairs={{0,1},{1,0},{2,3},{3,2},{4,5},{5,4},{6,7},{7,6},{8,9},{9,8},{10,11... | collective-permute-start | bytes 172040 | tf_op jit(solution)/shard_map/ppermute | solution.py:535
  104.3 3.8 %collective-permute-start.17 = (bf16[224,128]{1,0:T(8,128)(2,1)S(1)}, bf16[224,128]{1,0:T(8,128)(2,1)S(1)}, u32[]{:S(2)}, u32[]{:S(2)}) collective-permute-start(bf16[224,128]{1,0:T(8,128)(2,1)S(1)} %collective-permute-done.13.refs_2_), channel_id=1, source_target_pairs={{0,1},{1,0},{2,3},{3,2},{4,5},{5,4},{6,7},{7,6},{8,9},{9,8},{10,11... | collective-permute-start | bytes 172040 | tf_op jit(solution)/shard_map/ppermute | solution.py:535
  105.3 4.2 %collective-permute-start.32 = (bf16[272,128]{1,0:T(8,128)(2,1)S(1)}, bf16[272,128]{1,0:T(8,128)(2,1)S(1)}, u32[]{:S(2)}, u32[]{:S(2)}) collective-permute-start(bf16[272,128]{1,0:T(8,128)(2,1)S(1)} %slab_sum.3.refs_8_), channel_id=1, source_target_pairs={{0,1},{1,0},{2,3},{3,2},{4,5},{5,4},{6,7},{7,6},{8,9},{9,8},{10,11... | collective-permute-start | bytes 208904 | tf_op jit(solution)/shard_map/ppermute | solution.py:535
  106.1 3.3 %collective-permute-start.35 = (bf16[272,128]{1,0:T(8,128)(2,1)S(1)}, bf16[272,128]{1,0:T(8,128)(2,1)S(1)}, u32[]{:S(2)}, u32[]{:S(2)}) collective-permute-start(bf16[272,128]{1,0:T(8,128)(2,1)S(1)} %collective-permute-done.31.refs_11_), channel_id=1, source_target_pairs={{0,1},{1,0},{2,3},{3,2},{4,5},{5,4},{6,7},{7,6},{8,9},{9,8},{10,11... | collective-permute-start | bytes 208904 | tf_op jit(solution)/shard_map/ppermute | solution.py:535
  106.7 2.8 %collective-permute-start.34 = (bf16[272,128]{1,0:T(8,128)(2,1)S(1)}, bf16[272,128]{1,0:T(8,128)(2,1)S(1)}, u32[]{:S(2)}, u32[]{:S(2)}) collective-permute-start(bf16[272,128]{1,0:T(8,128)(2,1)S(1)} %collective-permute-done.30.refs_10_), channel_id=1, source_target_pairs={{0,1},{1,0},{2,3},{3,2},{4,5},{5,4},{6,7},{7,6},{8,9},{9,8},{10,11... | collective-permute-start | bytes 208904 | tf_op jit(solution)/shard_map/ppermute | solution.py:535
  108.0 1.4 %collective-permute-start.33 = (bf16[272,128]{1,0:T(8,128)(2,1)S(1)}, bf16[272,128]{1,0:T(8,128)(2,1)S(1)}, u32[]{:S(2)}, u32[]{:S(2)}) collective-permute-start(bf16[272,128]{1,0:T(8,128)(2,1)S(1)} %collective-permute-done.29.refs_9_), channel_id=1, source_target_pairs={{0,1},{1,0},{2,3},{3,2},{4,5},{5,4},{6,7},{7,6},{8,9},{9,8},{10,11... | collective-permute-start | bytes 208904 | tf_op jit(solution)/shard_map/ppermute | solution.py:535
  108.0 1.4 %collective-permute-start.16 = (bf16[224,128]{1,0:T(8,128)(2,1)S(1)}, bf16[224,128]{1,0:T(8,128)(2,1)S(1)}, u32[]{:S(2)}, u32[]{:S(2)}) collective-permute-start(bf16[224,128]{1,0:T(8,128)(2,1)S(1)} %collective-permute-done.12.refs_1_), channel_id=1, source_target_pairs={{0,1},{1,0},{2,3},{3,2},{4,5},{5,4},{6,7},{7,6},{8,9},{9,8},{10,11... | collective-permute-start | bytes 172040 | tf_op jit(solution)/shard_map/ppermute | solution.py:535
